TPU v7x, 32 devices: a whole 2x2x4 slice. The times are simulated.
32 devices in a mesh: wide: 8 (over z, x), narrow: 4 (over y, core).
Axes of the slice: x: 2, y: 2, z: 4, core: 2. Of those that a mesh axis runs over, the one named last changes fastest.
Arguments:
- images: bfloat16 [32, 16, 16, 2048], P(('wide', 'narrow')), may hold values from -18 to 18
- image_sizes: int32 [32, 2], P(('wide', 'narrow')), may hold values from 8 to 16
- offset_shift: int32 [18], replicated, may hold values from -24 to 24, as said below
- squeeze_one: bfloat16 [2048, 512], replicated, may hold values from -0.125 to 0.125
- offsets_one: bfloat16 [9, 512, 18], replicated, may hold values from -0.09375 to 0.09375
- spatial_one: bfloat16 [9, 512, 512], replicated, may hold values from -0.09375 to 0.09375
- expand_one: bfloat16 [512, 2048], replicated, may hold values from -0.25 to 0.25
- squeeze_two: bfloat16 [2048, 512], replicated, may hold values from -0.125 to 0.125
- spatial_two: bfloat16 [9, 512, 512], replicated, may hold values from -0.09375 to 0.09375
- expand_two: bfloat16 [512, 2048], replicated, may hold values from -0.25 to 0.25
- norm_gain_one: float32 [3072], replicated, may hold values from 0.5 to 1.5
- norm_bias_one: float32 [3072], replicated, may hold values from -1.5 to 1.5
- norm_gain_two: float32 [3072], replicated, may hold values from 0.5 to 1.5
- norm_bias_two: float32 [3072], replicated, may hold values from -1.5 to 1.5
- run_mean_one: float32 [3072], replicated, may hold values from -3 to 3
- run_var_one: float32 [3072], replicated, may hold values from 0.5 to 2
- run_mean_two: float32 [3072], replicated, may hold values from -3 to 3
- run_var_two: float32 [3072], replicated, may hold values from 0.5 to 2
- grad_output: bfloat16 [32, 16, 16, 2048], P(('wide', 'narrow')), may hold values from -6 to 6
Outputs:
- output_images: bfloat16 [32, 16, 16, 2048], P(('wide', 'narrow'))
- grad_images: bfloat16 [32, 16, 16, 2048], P(('wide', 'narrow'))
- grad_squeeze_one: float32 [2048, 512], P(None, 'wide')
- grad_offsets_one: float32 [9, 512, 18], replicated
- grad_spatial_one: float32 [9, 512, 512], P(None, 'wide')
- grad_expand_one: float32 [512, 2048], P('wide')
- grad_squeeze_two: float32 [2048, 512], P(None, 'wide')
- grad_spatial_two: float32 [9, 512, 512], P(None, 'wide')
- grad_expand_two: float32 [512, 2048], P('wide')
- grad_gain_one: float32 [3072], replicated
- grad_bias_one: float32 [3072], replicated
- grad_gain_two: float32 [3072], replicated
- grad_bias_two: float32 [3072], replicated
- new_mean_one: float32 [3072], replicated
- new_var_one: float32 [3072], replicated
- new_mean_two: float32 [3072], replicated
- new_var_two: float32 [3072], replicated
Inputs may be any that keep to these rules, and one draw needn't show every extreme that they name: `offset_shift`: every entry is -2 to 2 except the vertical shifts of two different taps, one 24 and the other -24.
All inputs are finite; a program needn't handle non-finite values.
Results may differ from a plain program's by a relative error of at most 0.024.
Values sent between devices are 32-bit elements; how exact they have to be, the bound alone decides.
No kernel may reach another device: no remote copies, remote signals or barrier semaphores. Data moves between devices by JAX's collectives and lax.ppermute only.
A program may use at most 192 MiB of HBM per device.

v0:
```python
import jax
import jax.numpy as jnp
from jax import lax
from jax.sharding import PartitionSpec as P

eps_norm = 1e-05
keep_rate = 0.6


def silu_slope(values):
    logistic = jax.nn.sigmoid(values)
    return logistic * (1.0 + values * (1.0 - logistic))


def dot_rows(first_op, second_op):
    return lax.dot_general(
        first_op, second_op, (((1,), (1,)), ((), ())), preferred_element_type=jnp.float32
    )


def dot_cols(first_op, second_op):
    return lax.dot_general(
        first_op, second_op, (((0,), (0,)), ((), ())), preferred_element_type=jnp.float32
    )


def split_low(values):
    upper = values.astype(jnp.bfloat16)
    lower = (values - upper.astype(jnp.float32)).astype(jnp.bfloat16)
    return (upper, lower)


def expand_taps(values, side_rows, side_cols):
    padded = jnp.pad(values, ((2, 2), (2, 2), (0, 0)))
    pieces = [
        padded[2 * tap_row : 2 * tap_row + side_rows, 2 * tap_col : 2 * tap_col + side_cols, :]
        for tap_row in range(3)
        for tap_col in range(3)
    ]
    return jnp.concatenate(pieces, axis=2).reshape(side_rows * side_cols, -1)


def fold_taps(grad_cols, side_rows, side_cols):
    channels = grad_cols.shape[1] // 9
    pieces = grad_cols.reshape(side_rows, side_cols, 9, channels)
    padded = jnp.zeros((side_rows + 4, side_cols + 4, channels), jnp.float32)
    for tap_index in range(9):
        tap_row, tap_col = (tap_index // 3, tap_index % 3)
        padded = padded.at[
            2 * tap_row : 2 * tap_row + side_rows, 2 * tap_col : 2 * tap_col + side_cols, :
        ].add(pieces[:, :, tap_index, :])
    return padded[2 : 2 + side_rows, 2 : 2 + side_cols, :].reshape(side_rows * side_cols, channels)


def tap_factors(offsets, tap_index, side_rows, side_cols):
    tap_row, tap_col = (tap_index // 3, tap_index % 3)
    position = jnp.arange(side_rows * side_cols, dtype=jnp.int32)
    row_base = (position // side_cols).astype(jnp.float32) + 2.0 * (tap_row - 1)
    col_base = (position % side_cols).astype(jnp.float32) + 2.0 * (tap_col - 1)
    dist_y = (row_base + offsets[:, 2 * tap_index])[:, None] - jnp.arange(
        side_rows, dtype=jnp.float32
    )[None, :]
    dist_x = (col_base + offsets[:, 2 * tap_index + 1])[:, None] - jnp.arange(
        side_cols, dtype=jnp.float32
    )[None, :]
    bump_y = jax.nn.relu(1.0 - dist_y * dist_y)
    bump_x = jax.nn.relu(1.0 - dist_x * dist_x)
    slope_y = -4.0 * dist_y * bump_y
    slope_x = -4.0 * dist_x * bump_x
    return (bump_y * bump_y, bump_x * bump_x, slope_y, slope_x)


def outer_rows(first_op, second_op):
    return (first_op[:, :, None] * second_op[:, None, :]).reshape(first_op.shape[0], -1)


def norm_finish(pre_norm, sum_values, squares, pixel_count, gain_part, bias_part):
    mean_value = sum_values / pixel_count
    var_value = squares / pixel_count - mean_value * mean_value
    inverse = lax.rsqrt(var_value + eps_norm)
    normed = (pre_norm - mean_value) * inverse
    return (gain_part * normed + bias_part, normed, inverse, mean_value, var_value)


def norm_forward(pre_norm, valid_mask, pixel_count, gain_part, bias_part):
    sum_values, squares = lax.psum(
        (jnp.sum(valid_mask * pre_norm, axis=0), jnp.sum(valid_mask * pre_norm * pre_norm, axis=0)),
        ("wide", "narrow"),
    )
    return norm_finish(pre_norm, sum_values, squares, pixel_count, gain_part, bias_part)


def norm_input_grad(
    grad_norm, normed, inverse, valid_mask, pixel_count, gain_part, sum_grad, sum_prod
):
    return (
        gain_part
        * inverse
        * (grad_norm - valid_mask * (sum_grad + normed * sum_prod) / pixel_count)
    )


def norm_backward(grad_norm, normed, inverse, valid_mask, pixel_count, gain_part):
    sum_grad, sum_prod = lax.psum(
        (jnp.sum(grad_norm, axis=0), jnp.sum(grad_norm * normed, axis=0)), ("wide", "narrow")
    )
    return (
        norm_input_grad(
            grad_norm, normed, inverse, valid_mask, pixel_count, gain_part, sum_grad, sum_prod
        ),
        sum_prod,
        sum_grad,
    )


def block_forward(
    inputs_low,
    residual,
    squeeze,
    spatial,
    expand,
    gain_all,
    bias_all,
    valid_mask,
    pixel_count,
    side_rows,
    side_cols,
    offset_weights,
    shift_float,
):
    middle = squeeze.shape[1]
    pre_first = jnp.dot(inputs_low, squeeze, preferred_element_type=jnp.float32)
    if pixel_count is None:
        sum_values, squares, pixel_count = lax.psum(
            (
                jnp.sum(valid_mask * pre_first, axis=0),
                jnp.sum(valid_mask * pre_first * pre_first, axis=0),
                jnp.sum(valid_mask),
            ),
            ("wide", "narrow"),
        )
        first_norm = norm_finish(
            pre_first, sum_values, squares, pixel_count, gain_all[:middle], bias_all[:middle]
        )
    else:
        first_norm = norm_forward(
            pre_first, valid_mask, pixel_count, gain_all[:middle], bias_all[:middle]
        )
    act_first = (jax.nn.silu(first_norm[0]) * valid_mask).astype(jnp.bfloat16)
    taps_first = expand_taps(act_first.reshape(side_rows, side_cols, middle), side_rows, side_cols)
    kept_values = {
        "inputs_low": inputs_low,
        "first": first_norm,
        "act_first": act_first,
        "taps_first": taps_first,
    }
    if offset_weights is None:
        columns = taps_first
    else:
        offsets = (
            jnp.dot(
                taps_first,
                offset_weights.reshape(9 * middle, -1),
                preferred_element_type=jnp.float32,
            )
            + shift_float
        )
        samples = []
        for tap_index in range(9):
            weight_y, weight_x, slope_y, slope_x = tap_factors(
                offsets, tap_index, side_rows, side_cols
            )
            sample_upper, sample_lower = split_low(outer_rows(weight_y, weight_x))
            samples.append(
                jnp.dot(sample_upper, act_first, preferred_element_type=jnp.float32)
                + jnp.dot(sample_lower, act_first, preferred_element_type=jnp.float32)
            )
        columns = jnp.concatenate(samples, axis=1).astype(jnp.bfloat16)
        kept_values["offsets"] = offsets
    pre_second = jnp.dot(
        columns, spatial.reshape(9 * middle, middle), preferred_element_type=jnp.float32
    )
    second_norm = norm_forward(
        pre_second,
        valid_mask,
        pixel_count,
        gain_all[middle : 2 * middle],
        bias_all[middle : 2 * middle],
    )
    act_second = (jax.nn.silu(second_norm[0]) * valid_mask).astype(jnp.bfloat16)
    pre_third = jnp.dot(act_second, expand, preferred_element_type=jnp.float32)
    third_norm = norm_forward(
        pre_third, valid_mask, pixel_count, gain_all[2 * middle :], bias_all[2 * middle :]
    )
    summed = third_norm[0] + residual
    kept_values["columns"] = columns
    kept_values["second"] = second_norm
    kept_values["act_second"] = act_second
    kept_values["third"] = third_norm
    kept_values["summed"] = summed
    means = jnp.concatenate([first_norm[3], second_norm[3], third_norm[3]])
    variances = jnp.concatenate([first_norm[4], second_norm[4], third_norm[4]])
    return (jax.nn.silu(summed) * valid_mask, kept_values, pixel_count, means, variances)


def block_backward(
    grad_result,
    kept_values,
    valid_mask,
    pixel_count,
    squeeze,
    spatial,
    expand,
    gain_all,
    offset_weights,
    side_rows,
    side_cols,
):
    middle = squeeze.shape[1]
    grad_sum = grad_result * valid_mask * silu_slope(kept_values["summed"])
    third = kept_values["third"]
    grad_third, prod_third, sum_third = norm_backward(
        grad_sum, third[1], third[2], valid_mask, pixel_count, gain_all[2 * middle :]
    )
    low_third = grad_third.astype(jnp.bfloat16)
    grad_expand = dot_cols(kept_values["act_second"], low_third)
    second = kept_values["second"]
    grad_act_second = dot_rows(low_third, expand) * valid_mask * silu_slope(second[0])
    grad_second, prod_second, sum_second = norm_backward(
        grad_act_second,
        second[1],
        second[2],
        valid_mask,
        pixel_count,
        gain_all[middle : 2 * middle],
    )
    low_second = grad_second.astype(jnp.bfloat16)
    spatial_flat = spatial.reshape(9 * middle, middle)
    grad_spatial = dot_cols(kept_values["columns"], low_second).reshape(9, middle, middle)
    grad_columns = dot_rows(low_second, spatial_flat)
    first = kept_values["first"]
    if offset_weights is None:
        grad_act_first = (
            fold_taps(grad_columns, side_rows, side_cols) * valid_mask * silu_slope(first[0])
        )
        grad_first, prod_first, sum_first = norm_backward(
            grad_act_first, first[1], first[2], valid_mask, pixel_count, gain_all[:middle]
        )
        grad_offsets = None
    else:
        offsets = kept_values["offsets"]
        act_first = kept_values["act_first"]
        grad_flat = jnp.zeros(act_first.shape, jnp.float32)
        slopes = []
        for tap_index in range(9):
            weight_y, weight_x, slope_y, slope_x = tap_factors(
                offsets, tap_index, side_rows, side_cols
            )
            sample_upper, sample_lower = split_low(outer_rows(weight_y, weight_x))
            piece_upper, piece_lower = split_low(
                grad_columns[:, tap_index * middle : (tap_index + 1) * middle]
            )
            grad_flat = (
                grad_flat
                + dot_cols(sample_upper, piece_upper)
                + dot_cols(sample_upper, piece_lower)
                + dot_cols(sample_lower, piece_upper)
            )
            product = dot_rows(piece_upper, act_first) + dot_rows(piece_lower, act_first)
            slopes.append(jnp.sum(product * outer_rows(slope_y, weight_x), axis=1))
            slopes.append(jnp.sum(product * outer_rows(weight_y, slope_x), axis=1))
        low_offsets = jnp.stack(slopes, axis=1).astype(jnp.bfloat16)
        grad_local = dot_cols(kept_values["taps_first"], low_offsets).reshape(9, middle, -1)
        back_taps = dot_rows(low_offsets, offset_weights.reshape(9 * middle, -1))
        grad_act_first = (
            (grad_flat + fold_taps(back_taps, side_rows, side_cols))
            * valid_mask
            * silu_slope(first[0])
        )
        sum_first, prod_first, grad_offsets = lax.psum(
            (
                jnp.sum(grad_act_first, axis=0),
                jnp.sum(grad_act_first * first[1], axis=0),
                grad_local,
            ),
            ("wide", "narrow"),
        )
        grad_first = norm_input_grad(
            grad_act_first,
            first[1],
            first[2],
            valid_mask,
            pixel_count,
            gain_all[:middle],
            sum_first,
            prod_first,
        )
    low_first = grad_first.astype(jnp.bfloat16)
    grad_squeeze = dot_cols(kept_values["inputs_low"], low_first)
    grad_input = grad_sum + dot_rows(low_first, squeeze)
    grad_gain = jnp.concatenate([prod_first, prod_second, prod_third])
    grad_bias = jnp.concatenate([sum_first, sum_second, sum_third])
    return (grad_input, grad_squeeze, grad_spatial, grad_expand, grad_offsets, grad_gain, grad_bias)


def sum_gradients(grad_squeeze, grad_spatial, grad_expand):
    partial_sums = (
        lax.psum_scatter(grad_squeeze, "wide", scatter_dimension=1, tiled=True),
        lax.psum_scatter(grad_spatial, "wide", scatter_dimension=1, tiled=True),
        lax.psum_scatter(grad_expand, "wide", scatter_dimension=0, tiled=True),
    )
    return lax.psum((partial_sums[0], partial_sums[1], partial_sums[2]), "narrow")


def per_device(
    images,
    image_sizes,
    offset_shift,
    squeeze_one,
    offsets_one,
    spatial_one,
    expand_one,
    squeeze_two,
    spatial_two,
    expand_two,
    norm_gain_one,
    norm_bias_one,
    norm_gain_two,
    norm_bias_two,
    run_mean_one,
    run_var_one,
    run_mean_two,
    run_var_two,
    grad_output,
):
    side_rows, side_cols, channels = (images.shape[1], images.shape[2], images.shape[3])
    pixels = side_rows * side_cols
    position = jnp.arange(pixels, dtype=jnp.int32)
    inside = (position // side_cols < image_sizes[0, 0]) & (
        position % side_cols < image_sizes[0, 1]
    )
    valid_mask = inside.astype(jnp.float32)[:, None]
    shift_float = offset_shift.astype(jnp.float32)
    inputs_low = images.reshape(pixels, channels)
    result_one, kept_one, pixel_count, means_one, vars_one = block_forward(
        inputs_low,
        inputs_low.astype(jnp.float32),
        squeeze_one,
        spatial_one,
        expand_one,
        norm_gain_one,
        norm_bias_one,
        valid_mask,
        None,
        side_rows,
        side_cols,
        offsets_one,
        shift_float,
    )
    result_two, kept_two, pixel_count, means_two, vars_two = block_forward(
        result_one.astype(jnp.bfloat16),
        result_one,
        squeeze_two,
        spatial_two,
        expand_two,
        norm_gain_two,
        norm_bias_two,
        valid_mask,
        pixel_count,
        side_rows,
        side_cols,
        None,
        shift_float,
    )
    grad_result = grad_output.reshape(pixels, channels).astype(jnp.float32)
    back_two = block_backward(
        grad_result,
        kept_two,
        valid_mask,
        pixel_count,
        squeeze_two,
        spatial_two,
        expand_two,
        norm_gain_two,
        None,
        side_rows,
        side_cols,
    )
    summed_two = sum_gradients(back_two[1], back_two[2], back_two[3])
    back_one = block_backward(
        back_two[0],
        kept_one,
        valid_mask,
        pixel_count,
        squeeze_one,
        spatial_one,
        expand_one,
        norm_gain_one,
        offsets_one,
        side_rows,
        side_cols,
    )
    summed_one = sum_gradients(back_one[1], back_one[2], back_one[3])
    unbias = pixel_count / (pixel_count - 1.0)
    new_mean_one = keep_rate * run_mean_one + (1.0 - keep_rate) * means_one
    new_var_one = keep_rate * run_var_one + (1.0 - keep_rate) * vars_one * unbias
    new_mean_two = keep_rate * run_mean_two + (1.0 - keep_rate) * means_two
    new_var_two = keep_rate * run_var_two + (1.0 - keep_rate) * vars_two * unbias
    output_images = result_two.astype(jnp.bfloat16).reshape(1, side_rows, side_cols, channels)
    grad_images = back_one[0].astype(jnp.bfloat16).reshape(1, side_rows, side_cols, channels)
    return (
        output_images,
        grad_images,
        summed_one[0],
        back_one[4],
        summed_one[1],
        summed_one[2],
        summed_two[0],
        summed_two[1],
        summed_two[2],
        back_one[5],
        back_one[6],
        back_two[5],
        back_two[6],
        new_mean_one,
        new_var_one,
        new_mean_two,
        new_var_two,
    )


def solution(mesh):
    placed = (
        P(("wide", "narrow"), None, None, None),
        P(("wide", "narrow"), None),
        P(),
        P(),
        P(),
        P(),
        P(),
        P(),
        P(),
        P(),
        P(),
        P(),
        P(),
        P(),
        P(),
        P(),
        P(),
        P(),
        P(("wide", "narrow"), None, None, None),
    )
    return jax.shard_map(
        per_device,
        mesh=mesh,
        in_specs=placed,
        out_specs=(
            P(("wide", "narrow"), None, None, None),
            P(("wide", "narrow"), None, None, None),
            P(None, "wide"),
            P(),
            P(None, "wide", None),
            P("wide", None),
            P(None, "wide"),
            P(None, "wide", None),
            P("wide", None),
            P(),
            P(),
            P(),
            P(),
            P(),
            P(),
            P(),
            P(),
        ),
        check_vma=False,
    )
```

profile of v0, /device:TPU:0, one launch (start us, length us, event | category | flops | bytes accessed | tf_op | source)
XLA Modules:
  0.0 1257.6 jit_solution(17815344750778016637)
XLA Ops:
  17.9 2.6 multiply_reduce_fusion.7
  20.6 42.3 %all-reduce.15 = (f32[512]{0:T(512)S(1)}, f32[]{:T(128)}, f32[512]{0:T(512)S(1)}) all-reduce(f32[512]{0:T(512)S(1)} %get-tuple-element.248, f32[]{:T(128)} %fusion.122, f32[512]{0:T(512)S(1)} %get-tuple-element.247), channel_id=1, replica_groups=mesh['wide'=8,'narrow'=4] {'wide','narrow'}, use_global_device_ids=true, to_apply=%region_5.6 | all-reduce | flops 1025 | bytes 8200 | tf_op jit(solution)/shard_map/psum | solution.py:134
  62.9 2.0 fusion.118
  85.3 2.2 multiply_reduce_fusion.6
  87.5 40.3 %all-reduce.14 = (f32[512]{0:T(512)S(1)}, f32[512]{0:T(512)S(1)}) all-reduce(f32[512]{0:T(512)S(1)} %get-tuple-element.246, f32[512]{0:T(512)S(1)} %get-tuple-element.245), channel_id=1, replica_groups=mesh['wide'=8,'narrow'=4] {'wide','narrow'}, use_global_device_ids=true, to_apply=%region_9.10 | all-reduce | flops 1024 | bytes 8192 | tf_op jit(solution)/shard_map/psum | solution.py:86
  127.8 2.0 fusion.119
  130.4 4.7 multiply_reduce_fusion.1
  135.1 40.3 %all-reduce.13 = (f32[2048]{0:T(1024)}, f32[2048]{0:T(1024)}) all-reduce(f32[2048]{0:T(1024)} %get-tuple-element.236, f32[2048]{0:T(1024)} %get-tuple-element.235), channel_id=1, replica_groups=mesh['wide'=8,'narrow'=4] {'wide','narrow'}, use_global_device_ids=true, to_apply=%region_13.14 | all-reduce | flops 4096 | bytes 32768 | tf_op jit(solution)/shard_map/psum | solution.py:86
  175.3 2.0 fusion.112
  178.0 2.6 multiply_multiply_fusion.2
  182.0 41.2 %all-reduce.12 = (f32[512]{0:T(512)S(1)}, f32[512]{0:T(512)S(1)}) all-reduce(f32[512]{0:T(512)S(1)} %get-tuple-element.244, f32[512]{0:T(512)S(1)} %get-tuple-element.243), channel_id=1, replica_groups=mesh['wide'=8,'narrow'=4] {'wide','narrow'}, use_global_device_ids=true, to_apply=%region_17.18 | all-reduce | flops 1024 | bytes 8192 | tf_op jit(solution)/shard_map/psum | solution.py:86
  223.2 2.0 fusion.120
  226.9 5.2 multiply_reduce_fusion.4
  232.1 40.2 %all-reduce.11 = (f32[512]{0:T(512)S(1)}, f32[512]{0:T(512)S(1)}) all-reduce(f32[512]{0:T(512)} %get-tuple-element.242, f32[512]{0:T(512)} %get-tuple-element.241), channel_id=1, replica_groups=mesh['wide'=8,'narrow'=4] {'wide','narrow'}, use_global_device_ids=true, to_apply=%region_21.22 | all-reduce | flops 1024 | bytes 8192 | tf_op jit(solution)/shard_map/psum | solution.py:86
  272.3 2.0 fusion.121
  274.8 2.8 multiply_reduce_fusion
  277.7 40.3 %all-reduce.10 = (f32[2048]{0:T(1024)S(1)}, f32[2048]{0:T(1024)S(1)}) all-reduce(f32[2048]{0:T(1024)S(1)} %get-tuple-element.234, f32[2048]{0:T(1024)S(1)} %get-tuple-element.233), channel_id=1, replica_groups=mesh['wide'=8,'narrow'=4] {'wide','narrow'}, use_global_device_ids=true, to_apply=%region_25.26 | all-reduce | flops 4096 | bytes 32768 | tf_op jit(solution)/shard_map/psum | solution.py:86
  319.9 5.7 fusion.128
  325.6 40.2 %all-reduce.9 = (f32[2048]{0:T(1024)}, f32[2048]{0:T(1024)}) all-reduce(f32[2048]{0:T(1024)S(1)} %get-tuple-element.240, f32[2048]{0:T(1024)S(1)} %get-tuple-element.239), channel_id=1, replica_groups=mesh['wide'=8,'narrow'=4] {'wide','narrow'}, use_global_device_ids=true, to_apply=%region_29.30 | all-reduce | flops 4096 | bytes 32768 | tf_op jit(solution)/shard_map/psum | solution.py:104
  365.8 3.6 multiply_convert_fusion.1
  369.5 2.8 fusion.125
  372.4 3.3 fusion.132
  375.7 43.3 %all-reduce.8 = (f32[512]{0:T(512)S(1)}, f32[512]{0:T(512)S(1)}) all-reduce(f32[512]{0:T(512)} %get-tuple-element.256, f32[512]{0:T(512)} %get-tuple-element.255), channel_id=1, replica_groups=mesh['wide'=8,'narrow'=4] {'wide','narrow'}, use_global_device_ids=true, to_apply=%region_33.34 | all-reduce | flops 1024 | bytes 8192 | tf_op jit(solution)/shard_map/psum | solution.py:104
  419.0 2.1 multiply_convert_fusion.6
  421.8 3.8 fusion
  427.7 2.0 add_select_fusion.3
  429.7 2.1 scatter-add.61
  432.4 3.0 add_select_fusion.2
  435.4 2.0 scatter-add.64
  446.0 2.0 fusion.43
  448.0 2.5 scatter-add.74
  452.0 39.6 %all-reduce.7 = (f32[512]{0:T(512)S(1)}, f32[512]{0:T(512)S(1)}) all-reduce(f32[512]{0:T(512)S(1)} %get-tuple-element.254, f32[512]{0:T(512)S(1)} %get-tuple-element.253), channel_id=1, replica_groups=mesh['wide'=8,'narrow'=4] {'wide','narrow'}, use_global_device_ids=true, to_apply=%region_39.40 | all-reduce | flops 1024 | bytes 8192 | tf_op jit(solution)/shard_map/psum | solution.py:104
  494.2 2.8 fusion.52
  498.8 5.8 fusion.127
  504.7 43.0 %all-reduce.6 = (f32[2048]{0:T(1024)S(1)}, f32[2048]{0:T(1024)S(1)}) all-reduce(f32[2048]{0:T(1024)} %get-tuple-element.238, f32[2048]{0:T(1024)} %get-tuple-element.237), channel_id=1, replica_groups=mesh['wide'=8,'narrow'=4] {'wide','narrow'}, use_global_device_ids=true, to_apply=%region_43.44 | all-reduce | flops 4096 | bytes 32768 | tf_op jit(solution)/shard_map/psum | solution.py:104
  547.7 3.7 multiply_convert_fusion
  551.4 2.8 fusion.123
  554.3 2.5 fusion.130
  556.8 41.5 %all-reduce.5 = (f32[512]{0:T(512)S(1)}, f32[512]{0:T(512)S(1)}) all-reduce(f32[512]{0:T(512)S(1)} %get-tuple-element.252, f32[512]{0:T(512)S(1)} %get-tuple-element.251), channel_id=1, replica_groups=mesh['wide'=8,'narrow'=4] {'wide','narrow'}, use_global_device_ids=true, to_apply=%region_47.48 | all-reduce | flops 1024 | bytes 8192 | tf_op jit(solution)/shard_map/psum | solution.py:104
  600.0 3.8 fusion.150
  607.3 2.0 fusion.60
  614.4 2.1 fusion.64
  619.8 2.1 fusion.66
  630.3 2.1 fusion.70
  642.5 3.4 fusion.85
  647.0 3.0 add_select_fusion.1
  650.2 2.1 scatter-add.76
  652.2 3.0 add_select_fusion
  655.2 2.0 scatter-add.79
  665.8 2.0 fusion.35
  667.7 2.8 scatter-add.89
  681.4 40.8 %all-reduce.4 = (f32[512]{0:T(512)S(1)}, f32[512]{0:T(512)S(1)}) all-reduce(f32[512]{0:T(512)S(1)} %get-tuple-element.250, f32[512]{0:T(512)S(1)} %get-tuple-element.249), channel_id=1, replica_groups=mesh['wide'=8,'narrow'=4] {'wide','narrow'}, use_global_device_ids=true, to_apply=%region_69.70 | all-reduce | flops 1024 | bytes 8192 | tf_op jit(solution)/shard_map/psum | solution.py:280
  723.0 2.8 convolution_bitcast_fusion
  727.5 5.1 fusion.161
  732.7 3.1 copy.92
  735.8 4.9 fusion.56
  742.5 2.4 copy.91
  745.0 3.2 fusion.110
  748.6 66.6 %reduce-scatter.7.cloned.1.call-done = f32[2048,64]{0,1:T(8,128)} async-done(((f32[2048,512]{0,1:T(8,128)}), f32[2048,64]{0,1:T(8,128)}) %reduce-scatter.7.cloned.1.call-update) | async-done | bytes 524304 | tf_op jit(solution)/shard_map/reduce_scatter | solution.py:308
  815.2 169.6 %reduce-scatter.9.cloned.1.call-done = f32[9,64,512]{2,1,0:T(8,128)} async-done(((f32[9,512,512]{2,1,0:T(8,128)}), f32[9,64,512]{2,1,0:T(8,128)}) %reduce-scatter.9.cloned.1.call-update) | async-done | bytes 1179664 | tf_op jit(solution)/shard_map/reduce_scatter | solution.py:309
  984.9 166.9 %reduce-scatter.15.cloned.1.call-done = f32[9,64,512]{2,1,0:T(8,128)} async-done(((f32[9,512,512]{2,1,0:T(8,128)}), f32[9,64,512]{2,1,0:T(8,128)}) %reduce-scatter.15.cloned.1.call-update) | async-done | bytes 1179664 | tf_op jit(solution)/shard_map/reduce_scatter | solution.py:309
  1155.9 3.7 fusion.4
  1159.6 81.8 %all-reduce.22.cloned.1.call-done = (f32[2048,64]{0,1:T(8,128)}, f32[9,64,512]{2,1,0:T(8,128)}, f32[64,2048]{1,0:T(8,128)}, f32[2048,64]{0,1:T(8,128)}, f32[9,64,512]{2,1,0:T(8,128)}, /*index=5*/f32[64,2048]{1,0:T(8,128)}) async-done(((f32[2048,64]{0,1:T(8,128)}, f32[9,64,512]{2,1,0:T(8,128)}, f32[64,2048]{1,0:T(8,128)}, f32[2048,64]{0,1:T(8,128)}, f32[9,64,512]{2,1,0:T(8,128)}, ...) | async-done | bytes 4456464 | tf_op jit(solution)/shard_map/psum | solution.py:312
  1241.4 2.0 copy.154
  (623 shorter events, 119.2 us)
Async XLA Ops:
  8.0 266.8 %copy-start = (bf16[512,2048]{1,0:T(8,128)(2,1)S(1)}, bf16[512,2048]{1,0:T(8,128)(2,1)}, u32[]{:S(2)}) copy-start(bf16[512,2048]{1,0:T(8,128)(2,1)} %param.64) | copy-start | bytes 6291460
  8.0 740.5 %reduce-scatter.17.cloned.1.call-start = ((), (), s32[]{:S(2)}) async-start(), calls=%async_computation.12 | async-start | bytes 4718592 | tf_op jit(solution)/shard_map/reduce_scatter | solution.py:310
  13.4 52.6 %copy-start.127 = (f32[512]{0:T(512)}, f32[512]{0:T(512)S(1)}, u32[]{:S(2)}) copy-start(f32[512]{0:T(512)S(1)} %get-tuple-element.419) | copy-start | bytes 6148
  13.4 116.9 %copy-start.104 = (f32[512]{0:T(512)}, f32[512]{0:T(512)S(1)}, u32[]{:S(2)}) copy-start(f32[512]{0:T(512)S(1)} %get-tuple-element.418) | copy-start | bytes 6148
  20.6 45.5 %copy-start.17 = (f32[256,512]{1,0:T(8,128)}, f32[256,512]{1,0:T(8,128)S(1)}, u32[]{:S(2)}) copy-start(f32[256,512]{1,0:T(8,128)S(1)} %get-tuple-element.469) | copy-start | bytes 1572868
  68.5 14.4 %copy-start.49 = (bf16[256,256]{0,1:T(8,128)(2,1)}, bf16[256,256]{0,1:T(8,128)(2,1)S(1)}, u32[]{:S(2)}) copy-start(bf16[256,256]{0,1:T(8,128)(2,1)S(1)} %get-tuple-element.338) | copy-start | bytes 393220
  69.7 13.5 %copy-start.51 = (bf16[256,256]{0,1:T(8,128)(2,1)}, bf16[256,256]{0,1:T(8,128)(2,1)S(1)}, u32[]{:S(2)}) copy-start(bf16[256,256]{0,1:T(8,128)(2,1)S(1)} %get-tuple-element.336) | copy-start | bytes 393220
  71.4 12.0 copy-start.53
  73.2 10.5 copy-start.55
  75.0 8.9 copy-start.57
  76.9 7.4 copy-start.59
  78.6 5.8 copy-start.61
  130.4 47.6 %copy-start.21 = (bf16[1,16,16,2048]{3,2,1,0:T(8,128)(2,1)S(1)}, bf16[1,16,16,2048]{3,2,1,0:T(8,128)(2,1)}, u32[]{:S(2)}) copy-start(bf16[1,16,16,2048]{3,2,1,0:T(8,128)(2,1)} %param.55) | copy-start | bytes 3145732
  180.6 45.1 %copy-start.115 = (f32[512]{0:T(512)S(1)}, f32[512]{0:T(512)}, u32[]{:S(2)}) copy-start(f32[512]{0:T(512)} %get-tuple-element.414) | copy-start | bytes 6148
  182.0 50.1 %copy-start.5 = (f32[256,512]{1,0:T(8,128)}, f32[256,512]{1,0:T(8,128)S(1)}, u32[]{:S(2)}) copy-start(f32[256,512]{1,0:T(8,128)S(1)} %get-tuple-element.472) | copy-start | bytes 1572868
  232.1 45.6 %copy-start.25 = (f32[256,512]{1,0:T(8,128)}, f32[256,512]{1,0:T(8,128)S(1)}, u32[]{:S(2)}) copy-start(f32[256,512]{1,0:T(8,128)S(1)} %get-tuple-element.473) | copy-start | bytes 1572868
  274.8 43.2 %copy-start.143 = (f32[3072]{0:T(1024)S(1)}, f32[3072]{0:T(1024)}, u32[]{:S(2)}) copy-start(f32[3072]{0:T(1024)} %param.67) | copy-start | bytes 36868
  274.8 45.1 %slice-start.4 = ((f32[3072]{0:T(1024)}), f32[2048]{0:T(1024)S(1)}, s32[]{:S(2)}) async-start(f32[3072]{0:T(1024)} %param.68), calls=%async_computation.18 | async-start | bytes 16384 | tf_op jit(solution)/shard_map/slice | solution.py:193
  319.3 6.3 copy-start.84
  319.9 5.7 copy-start.101
  372.3 376.3 %reduce-scatter.13.cloned.1.call-start = ((), (), s32[]{:S(2)}) async-start(), calls=%async_computation.10 | async-start | bytes 4718592 | tf_op jit(solution)/shard_map/reduce_scatter | solution.py:308
  419.0 6.5 copy-start.144
  419.0 6.5 copy-start.146
  446.0 45.6 %copy-start.158 = (f32[512]{0:T(512)S(1)}, f32[512]{0:T(512)}, u32[]{:S(2)}) copy-start(f32[512]{0:T(512)} %get-tuple-element.314) | copy-start | bytes 6148
  448.0 46.3 %copy-start.4 = (f32[256,2048]{1,0:T(8,128)S(1)}, f32[256,2048]{1,0:T(8,128)}, u32[]{:S(2)}) copy-start(f32[256,2048]{1,0:T(8,128)} %copy-done.3) | copy-start | bytes 6291460
  497.0 251.6 %reduce-scatter.11.cloned.1.call-start = ((), (), s32[]{:S(2)}) async-start(), calls=%async_computation.9 | async-start | bytes 4718592 | tf_op jit(solution)/shard_map/reduce_scatter | solution.py:310
  554.3 44.1 %copy-start.157 = (f32[512]{0:T(512)S(1)}, f32[512]{0:T(512)}, u32[]{:S(2)}) copy-start(f32[512]{0:T(512)} %get-tuple-element.310) | copy-start | bytes 6148
  554.3 260.9 %reduce-scatter.7.cloned.1.call-start = ((), (), s32[]{:S(2)}) async-start(), calls=%async_computation.6 | async-start | bytes 4718592 | tf_op jit(solution)/shard_map/reduce_scatter | solution.py:308
  604.1 26.2 %copy-start.8 = (bf16[256,512]{1,0:T(8,128)(2,1)}, bf16[256,512]{1,0:T(8,128)(2,1)S(1)}, u32[]{:S(2)}) copy-start(bf16[256,512]{1,0:T(8,128)(2,1)S(1)} %get-tuple-element.346) | copy-start | bytes 786436
  604.1 31.5 %copy-start.10 = (bf16[256,512]{1,0:T(8,128)(2,1)}, bf16[256,512]{1,0:T(8,128)(2,1)S(1)}, u32[]{:S(2)}) copy-start(bf16[256,512]{1,0:T(8,128)(2,1)S(1)} %get-tuple-element.347) | copy-start | bytes 786436
  614.4 10.7 copy-start.67
  614.4 10.7 copy-start.68
  630.2 9.0 copy-start.65
  630.2 9.0 copy-start.66
  667.7 6.9 slice-start
  680.6 41.6 %copy-start.156 = (f32[512]{0:T(512)S(1)}, f32[512]{0:T(512)}, u32[]{:S(2)}) copy-start(f32[512]{0:T(512)} %get-tuple-element.308) | copy-start | bytes 6148
  680.9 42.1 %copy-start.23 = (bf16[1,16,16,2048]{3,2,1,0:T(8,128)(2,1)S(1)}, bf16[1,16,16,2048]{3,2,1,0:T(8,128)(2,1)}, u32[]{:S(2)}) copy-start(bf16[1,16,16,2048]{3,2,1,0:T(8,128)(2,1)} %param.55) | copy-start | bytes 3145732
  725.8 259.0 %reduce-scatter.9.cloned.1.call-start = ((), (), s32[]{:S(2)}) async-start(), calls=%async_computation.8 | async-start | bytes 10616832 | tf_op jit(solution)/shard_map/reduce_scatter | solution.py:309
  732.6 419.1 %reduce-scatter.15.cloned.1.call-start = ((), (), s32[]{:S(2)}) async-start(), calls=%async_computation.11 | async-start | bytes 10616832 | tf_op jit(solution)/shard_map/reduce_scatter | solution.py:309
  740.9 418.7 %all-reduce.20.cloned.1.call-start = ((), (), s32[]{:S(2)}) async-start(), calls=%async_computation.7 | async-start | bytes 884736 | tf_op jit(solution)/shard_map/psum | solution.py:280
  748.2 405.1 %copy-start.121 = (f32[2048]{0:T(1024)S(1)}, f32[2048]{0:T(1024)}, u32[]{:S(2)}) copy-start(f32[2048]{0:T(1024)} %get-tuple-element.287) | copy-start | bytes 24580
  748.2 405.1 %copy-start.122 = (f32[2048]{0:T(1024)S(1)}, f32[2048]{0:T(1024)}, u32[]{:S(2)}) copy-start(f32[2048]{0:T(1024)} %get-tuple-element.288) | copy-start | bytes 24580
  748.2 405.1 %copy-start.145 = (f32[512]{0:T(512)S(1)}, f32[512]{0:T(512)}, u32[]{:S(2)}) copy-start(f32[512]{0:T(512)} %copy-done.144) | copy-start | bytes 6148
  748.2 405.1 %copy-start.147 = (f32[512]{0:T(512)S(1)}, f32[512]{0:T(512)}, u32[]{:S(2)}) copy-start(f32[512]{0:T(512)} %copy-done.146) | copy-start | bytes 6148
  748.3 405.1 %copy-start.149 = (f32[512]{0:T(512)S(1)}, f32[512]{0:T(512)}, u32[]{:S(2)}) copy-start(f32[512]{0:T(512)} %copy-done.148) | copy-start | bytes 6148
  748.3 405.1 %copy-start.151 = (f32[512]{0:T(512)S(1)}, f32[512]{0:T(512)}, u32[]{:S(2)}) copy-start(f32[512]{0:T(512)} %copy-done.150) | copy-start | bytes 6148
  748.3 405.7 %copy-start.124 = (f32[2048]{0:T(1024)S(1)}, f32[2048]{0:T(1024)}, u32[]{:S(2)}) copy-start(f32[2048]{0:T(1024)} %copy-done.123) | copy-start | bytes 24580
  748.3 405.7 %copy-start.126 = (f32[2048]{0:T(1024)S(1)}, f32[2048]{0:T(1024)}, u32[]{:S(2)}) copy-start(f32[2048]{0:T(1024)} %copy-done.125) | copy-start | bytes 24580
  748.3 405.7 %copy-start.153 = (f32[512]{0:T(512)S(1)}, f32[512]{0:T(512)}, u32[]{:S(2)}) copy-start(f32[512]{0:T(512)} %copy-done.152) | copy-start | bytes 6148
  748.3 405.6 %copy-start.155 = (f32[512]{0:T(512)S(1)}, f32[512]{0:T(512)}, u32[]{:S(2)}) copy-start(f32[512]{0:T(512)} %copy-done.154) | copy-start | bytes 6148
  748.3 406.3 %copy-start.98 = (f32[2048]{0:T(1024)S(1)}, f32[2048]{0:T(1024)}, u32[]{:S(2)}) copy-start(f32[2048]{0:T(1024)} %copy-done.97) | copy-start | bytes 24580
  748.4 406.3 %copy-start.132 = (f32[512]{0:T(512)S(1)}, f32[512]{0:T(512)}, u32[]{:S(2)}) copy-start(f32[512]{0:T(512)} %copy-done.131) | copy-start | bytes 6148
  748.4 406.2 %copy-start.134 = (f32[512]{0:T(512)S(1)}, f32[512]{0:T(512)}, u32[]{:S(2)}) copy-start(f32[512]{0:T(512)} %copy-done.133) | copy-start | bytes 6148
  748.4 406.2 %copy-start.139 = (f32[3072]{0:T(1024)S(1)}, f32[3072]{0:T(1024)}, u32[]{:S(2)}) copy-start(f32[3072]{0:T(1024)} %param.69) | copy-start | bytes 36868
  748.4 406.2 %copy-start.140 = (f32[3072]{0:T(1024)S(1)}, f32[3072]{0:T(1024)}, u32[]{:S(2)}) copy-start(f32[3072]{0:T(1024)} %param.70) | copy-start | bytes 36868
  748.4 406.9 %copy-start.85 = (f32[2048]{0:T(1024)S(1)}, f32[2048]{0:T(1024)}, u32[]{:S(2)}) copy-start(f32[2048]{0:T(1024)} %copy-done.84) | copy-start | bytes 24580
  748.4 406.8 %copy-start.88 = (f32[512]{0:T(512)S(1)}, f32[512]{0:T(512)}, u32[]{:S(2)}) copy-start(f32[512]{0:T(512)} %copy-done.86) | copy-start | bytes 6148
  748.4 406.8 %copy-start.96 = (f32[512]{0:T(512)S(1)}, f32[512]{0:T(512)}, u32[]{:S(2)}) copy-start(f32[512]{0:T(512)} %copy-done.94) | copy-start | bytes 6148
  748.4 406.8 %copy-start.100 = (f32[2048]{0:T(1024)S(1)}, f32[2048]{0:T(1024)}, u32[]{:S(2)}) copy-start(f32[2048]{0:T(1024)} %copy-done.99) | copy-start | bytes 24580
  748.4 406.8 %copy-start.136 = (f32[512]{0:T(512)S(1)}, f32[512]{0:T(512)}, u32[]{:S(2)}) copy-start(f32[512]{0:T(512)} %copy-done.135) | copy-start | bytes 6148
  748.5 406.8 %copy-start.138 = (f32[512]{0:T(512)S(1)}, f32[512]{0:T(512)}, u32[]{:S(2)}) copy-start(f32[512]{0:T(512)} %copy-done.137) | copy-start | bytes 6148
  748.5 406.8 %copy-start.141 = (f32[3072]{0:T(1024)S(1)}, f32[3072]{0:T(1024)}, u32[]{:S(2)}) copy-start(f32[3072]{0:T(1024)} %param.71) | copy-start | bytes 36868
  748.5 406.8 %copy-start.142 = (f32[3072]{0:T(1024)S(1)}, f32[3072]{0:T(1024)}, u32[]{:S(2)}) copy-start(f32[3072]{0:T(1024)} %param.72) | copy-start | bytes 36868
  748.5 492.9 %all-reduce.22.cloned.1.call-start = ((), (), s32[]{:S(2)}) async-start(), calls=%async_computation.13 | async-start | bytes 8912896 | tf_op jit(solution)/shard_map/psum | solution.py:312
  (136 other events, 290.5 us)
Sparse Core Ops, SparseCore 0:
  372.4 89.9 reduce-scatter.16
  497.1 90.6 reduce-scatter.12
  591.9 87.8 reduce-scatter.10
  725.9 89.2 reduce-scatter.6
  819.1 165.7 reduce-scatter.8
  988.8 162.9 reduce-scatter.14
Sparse Core Ops, SparseCore 1:
  748.4 192.8 all-reduce.19
  1151.9 89.5 all-reduce.21
where the time goes:
time: 1270 us; the launch traced here: 1260 us
  blocking collectives  493 us (39%)
  waiting for transfers between devices  485 us (38%)
  matrix products  99.7 us (8%)
  local copies, waits for them, and re-layouts  81.8 us (6%)
  other arithmetic  77.1 us (6%)
  between operations  20.6 us (2%)
    reduce_scatter x2, waiting for transfers between devices, sum_gradients(): lax.psum_scatter(grad_spatial, 'wide', scatter_dimension=1, tiled=True)  337 us
    psum x5, blocking collectives, norm_backward(): lax.psum((jnp.sum(grad_norm, axis=0), jnp.sum(grad_norm * normed, axis=0)...  208 us
    psum x5, blocking collectives, norm_forward(): lax.psum((jnp.sum(valid_mask * pre_norm, axis=0), jnp.sum(valid_mask * pr...  202 us
    psum x1, waiting for transfers between devices, sum_gradients(): lax.psum((partial_sums[0], partial_sums[1], partial_sums[2]), 'narrow')  81.8 us
    reduce_scatter x2, waiting for transfers between devices, sum_gradients(): lax.psum_scatter(grad_squeeze, 'wide', scatter_dimension=1, tiled=True)  66.6 us
    dot_general x25, matrix products, dot_rows(): lax.dot_general(first_op, second_op, (((1,), (1,)), ((), ())), preferred_...  43.3 us
    psum x1, blocking collectives, block_forward(): lax.psum((jnp.sum(valid_mask * pre_first, axis=0), jnp.sum(valid_mask * p...  42.3 us
    psum x1, blocking collectives, block_backward(): lax.psum((jnp.sum(grad_act_first, axis=0), jnp.sum(grad_act_first * first...  40.8 us
  transfers between devices with their start and end apart: 8, of which 4 were waited for; matrix products, arithmetic and copies ran while one was open for 13% of the time, Pallas kernels for 0%

commit v1 on v0

v1 whole, which is shorter than its diff:
```python
import functools

import jax
import jax.numpy as jnp
from jax import lax
from jax.experimental import pallas as pl
from jax.experimental.pallas import tpu as pltpu
from jax.sharding import PartitionSpec as P

eps_norm = 1e-05
keep_rate = 0.6
vmem_bytes = 60 * 1024 * 1024
lane = 128
tile_rows = 16
axes = ("wide", "narrow")
f32 = jnp.float32
bf16 = jnp.bfloat16


def shape_of(shape, kind=f32):
    return jax.ShapeDtypeStruct(shape, kind)


copies_of = {}


def need(ref):
    entry = copies_of.get(id(ref))
    if entry is not None and entry[1]:
        entry[1] = False
        entry[0].wait()
    return ref


def flush(ref):
    entry = copies_of.get(id(ref))
    if entry is not None and entry[1]:
        entry[1] = False
        entry[0].start()


def call(body, outs, args, smem=(), scratch=(), after=(), late=(), stay=None, stay_out=()):
    stay = () if stay is None else stay
    hbm = pl.BlockSpec(memory_space=pltpu.HBM)
    vmem = pl.BlockSpec(memory_space=pltpu.VMEM)
    specs = [
        pl.BlockSpec(memory_space=pltpu.SMEM) if place in smem else vmem if place in stay else hbm
        for place in range(len(args))
    ] + [pl.BlockSpec(memory_space=pl.ANY)] * len(after)
    moved = [place for place in range(len(args)) if place not in smem and place not in stay]
    used, extra, made = (len(args), len(after), len(outs))
    sent = [slot for slot in range(made) if slot not in stay_out]

    def kernel(*refs):
        given = list(refs[:used])
        results = list(refs[used + extra : used + extra + made])
        rest = refs[used + extra + made :]
        in_slots, out_slots = (rest[: len(moved)], rest[len(moved) : len(moved) + len(sent)])
        in_flags, out_flags = rest[len(moved) + len(sent) : len(moved) + len(sent) + 2]
        copies_of.clear()
        for slot, place in enumerate(moved):
            copy = pltpu.make_async_copy(given[place], in_slots[slot], in_flags.at[slot])
            copy.start()
            copies_of[id(in_slots[slot])] = [copy, True]
            given[place] = in_slots[slot]
        for place in moved:
            if place not in late:
                need(given[place])
        for slot, place in enumerate(sent):
            copies_of[id(out_slots[slot])] = [
                pltpu.make_async_copy(out_slots[slot], results[place], out_flags.at[slot]), True
            ]
            results[place] = out_slots[slot]
        body(*given, *results, *rest[len(moved) + len(sent) + 2 :])
        for place in moved:
            need(given[place])
        for slot in out_slots:
            if copies_of[id(slot)][1]:
                flush(slot)
        for slot in out_slots:
            copies_of[id(slot)][0].wait()
        copies_of.clear()

    slots = [pltpu.VMEM(args[place].shape, args[place].dtype) for place in moved]
    slots += [pltpu.VMEM(outs[place].shape, outs[place].dtype) for place in sent]
    flags = [pltpu.SemaphoreType.DMA((max(len(moved), 1),)), pltpu.SemaphoreType.DMA((max(len(sent), 1),))]
    return pl.pallas_call(
        kernel,
        out_shape=tuple(outs),
        in_specs=specs,
        out_specs=tuple(vmem if place in stay_out else hbm for place in range(made)),
        scratch_shapes=slots + flags + list(scratch),
        compiler_params=pltpu.CompilerParams(vmem_limit_bytes=vmem_bytes),
    )(*args, *after)


def dot_nn(first_op, second_op):
    return lax.dot_general(
        first_op, second_op, (((1,), (0,)), ((), ())), preferred_element_type=f32
    )


def dot_nt(first_op, second_op):
    return lax.dot_general(
        first_op, second_op, (((1,), (1,)), ((), ())), preferred_element_type=f32
    )


def dot_tn(first_op, second_op):
    return lax.dot_general(
        first_op, second_op, (((0,), (0,)), ((), ())), preferred_element_type=f32
    )


def logistic(values):
    return 0.5 * jnp.tanh(0.5 * values) + 0.5


def silu(values):
    return values * logistic(values)


def silu_slope(values):
    gate = logistic(values)
    return gate * (1.0 + values * (1.0 - gate))


def flat_row(rows, start, width):
    first = start // lane
    return jnp.concatenate(
        [rows[first + step : first + step + 1, :] for step in range(width // lane)], axis=1
    )


def fold_row(row):
    return [row[:, step * lane : (step + 1) * lane] for step in range(row.shape[1] // lane)]


def write_copies(copies_ref, rows, extra=None):
    packed = jnp.concatenate([piece for row in rows for piece in fold_row(row)], axis=0)
    if extra is not None:
        packed = jnp.concatenate([packed, extra], axis=0)

    def one_copy(step, carry):
        copies_ref[step] = packed
        return carry

    lax.fori_loop(0, copies_ref.shape[0], one_copy, 0)


def read_copies(copies_ref):
    return jnp.sum(copies_ref[...], axis=0)


def wide_mask(mask_ref, rows, width):
    return jnp.concatenate([mask_ref[rows, :]] * (width // lane), axis=1)


def eight_rows(values):
    folded = values[:8]
    for start in range(8, values.shape[0], 8):
        folded = folded + values[start : start + 8]
    return folded


def row_loop(pixels, body, carry):
    def step(index, state):
        return body(pl.ds(pl.multiple_of(index * tile_rows, tile_rows), tile_rows), state)

    return lax.fori_loop(0, pixels // tile_rows, step, carry)


def two_sums(pixels, width, body):
    zero = jnp.zeros((8, width), f32)

    def step(rows, state):
        first, second = body(rows)
        return (state[0] + eight_rows(first), state[1] + eight_rows(second))

    first, second = row_loop(pixels, step, (zero, zero))
    return (jnp.sum(first, axis=0, keepdims=True), jnp.sum(second, axis=0, keepdims=True))


def moments(total, width, count):
    mean = flat_row(total, 0, width) / count
    var = flat_row(total, width, width) / count - mean * mean
    return (mean, var)


def scale_shift(mean, var, gain, bias):
    inverse = lax.rsqrt(var + eps_norm)
    scale = gain * inverse
    return (scale, bias - mean * scale)


def spans_of(width, block):
    return [(start, min(block, width - start)) for start in range(0, width, block)]


def grad_rows(total, stats, gain, count, width):
    mean, var = (stats[0:1], stats[1:2])
    inverse = lax.rsqrt(var + eps_norm)
    sum_grad = flat_row(total, 0, width)
    sum_prod = flat_row(total, width, width)
    return (
        gain * inverse,
        sum_grad / count,
        inverse * sum_prod / count,
        mean,
        sum_grad,
        sum_prod,
    )


def build_taps(act_ref, shifted_ref, pixels, side):
    pad = 2 * side
    width = act_ref.shape[1]
    column = lax.broadcasted_iota(jnp.int32, (pixels, lane), 0) % side
    for tap_col in range(3):
        move = 2 * (tap_col - 1)
        moved = act_ref[pl.ds(pad + move, pixels), :]
        if move:
            inside = (column + move >= 0) & (column + move < side)
            keep = jnp.concatenate([inside.astype(f32)] * (width // lane), axis=1)
            moved = moved * keep
        shifted_ref[tap_col, pl.ds(0, pad), :] = jnp.zeros((pad, width), bf16)
        shifted_ref[tap_col, pl.ds(pad + pixels, pad), :] = jnp.zeros((pad, width), bf16)
        shifted_ref[tap_col, pl.ds(pad, pixels), :] = moved.astype(bf16)


def tap_of(shifted_ref, tap_index, pixels, side):
    tap_row, tap_col = (tap_index // 3, tap_index % 3)
    return shifted_ref[tap_col, pl.ds(2 * side * tap_row, pixels), :]


def fold_columns(sums_ref, pixels, side):
    pad = 2 * side
    width = sums_ref.shape[2]
    column = lax.broadcasted_iota(jnp.int32, (pixels, lane), 0) % side
    total = sums_ref[1, pl.ds(pad, pixels), :]
    for tap_col in (0, 2):
        move = 2 * (tap_col - 1)
        inside = (column - move >= 0) & (column - move < side)
        keep = jnp.concatenate([inside.astype(f32)] * (width // lane), axis=1)
        total = total + keep * sums_ref[tap_col, pl.ds(pad - move, pixels), :]
    return total


def tap_rows_out(sums_ref, tap_index, pixels, side, values):
    tap_row, tap_col = (tap_index // 3, tap_index % 3)
    rows = pl.ds(2 * side * tap_row, pixels)
    sums_ref[tap_col, rows, :] = sums_ref[tap_col, rows, :] + values


def tap_factors(offsets, tap_index, side):
    pixels = offsets.shape[0]
    tap_row, tap_col = (tap_index // 3, tap_index % 3)
    shape = (pixels, pixels)
    position = lax.broadcasted_iota(jnp.int32, shape, 0)
    source = lax.broadcasted_iota(jnp.int32, shape, 1)
    gap_y = (position // side - source // side + 2 * (tap_row - 1)).astype(f32)
    gap_x = (position % side - source % side + 2 * (tap_col - 1)).astype(f32)
    dist_y = gap_y + offsets[:, 2 * tap_index : 2 * tap_index + 1]
    dist_x = gap_x + offsets[:, 2 * tap_index + 1 : 2 * tap_index + 2]
    bump_y = jnp.maximum(1.0 - dist_y * dist_y, 0.0)
    bump_x = jnp.maximum(1.0 - dist_x * dist_x, 0.0)
    return (dist_y, dist_x, bump_y, bump_x)


def first_body(sizes_ref, place_ref, images_ref, squeeze_ref, pre_ref, mask_ref, copies_ref, half_ref):
    pixels, width = pre_ref.shape
    side = 1 << ((pixels.bit_length() - 1) // 2)
    position = lax.broadcasted_iota(jnp.int32, (pixels, lane), 0)
    inside = (position // side < sizes_ref[0, 0]) & (position % side < sizes_ref[0, 1])
    mask = inside.astype(f32)
    mask_ref[...] = mask
    pre_ref[...] = dot_nn(images_ref[...], squeeze_ref[...])

    def both(rows):
        values = pre_ref[rows, :]
        masked = values * wide_mask(mask_ref, rows, width)
        return (masked, masked * values)

    sums = two_sums(pixels, width, both)
    amount = jnp.sum(mask, axis=0, keepdims=True)
    write_copies(copies_ref, sums, jnp.broadcast_to(amount, (8, lane)))
    half = half_ref.shape[1]
    other = pl.multiple_of((1 - place_ref[0, 0]) * half, lane)
    half_ref[...] = images_ref[:, pl.ds(other, half)].astype(f32)


def activate(pre_ref, mask_ref, scale, shift, out_ref, base=0):
    pixels, width = pre_ref.shape

    def step(rows, carry):
        out = silu(pre_ref[rows, :] * scale + shift) * wide_mask(mask_ref, rows, width)
        target = pl.ds(rows.start + base, tile_rows)
        out_ref[target, :] = out.astype(bf16).astype(out_ref.dtype)
        return carry

    row_loop(pixels, step, 0)


def masked_sums(values_ref, mask_ref):
    pixels, width = values_ref.shape

    def both(rows):
        values = values_ref[rows, :]
        masked = values * wide_mask(mask_ref, rows, width)
        return (masked, masked * values)

    return two_sums(pixels, width, both)


def deform_body(
    total_ref, pre_ref, mask_ref, gain_ref, bias_ref, weights_ref, move_ref, spatial_ref,
    act_ref, columns_ref, columns_wide_ref, offsets_ref, second_ref, copies_ref, stats_ref,
    count_ref, padded_ref, shifted_ref,
):
    pixels, width = pre_ref.shape
    side = 1 << ((pixels.bit_length() - 1) // 2)
    total = read_copies(total_ref)
    count = total[2 * width // lane : 2 * width // lane + 1, 0:1]
    count_ref[...] = jnp.broadcast_to(count, (8, lane))
    mean, var = moments(total, width, count)
    stats_ref[...] = jnp.concatenate([mean, var], axis=0)
    scale, shift = scale_shift(mean, var, gain_ref[:, :width], bias_ref[:, :width])
    padded_ref[...] = jnp.zeros_like(padded_ref)
    activate(pre_ref, mask_ref, scale, shift, padded_ref, 2 * side)
    act_ref[...] = padded_ref[pl.ds(2 * side, pixels), :].astype(bf16)
    build_taps(padded_ref, shifted_ref, pixels, side)
    flush(act_ref)
    offsets = move_ref[...]
    need(weights_ref)
    for tap_index in range(9):
        taps = tap_of(shifted_ref, tap_index, pixels, side)
        offsets = offsets + dot_nn(taps, weights_ref[tap_index])
    offsets_ref[...] = offsets
    flush(offsets_ref)
    need(spatial_ref)
    second_ref[...] = jnp.zeros_like(second_ref)
    for tap_index in range(9):
        dist_y, dist_x, bump_y, bump_x = tap_factors(offsets, tap_index, side)
        root = bump_y * bump_x
        columns = dot_nn((root * root).astype(bf16), act_ref[...]).astype(bf16)
        span = pl.ds(tap_index * width, width)
        columns_ref[:, span] = columns
        columns_wide_ref[:, span] = columns.astype(f32)
        second_ref[...] = second_ref[...] + dot_nn(columns, spatial_ref[tap_index])
    flush(columns_wide_ref)
    flush(columns_ref)
    write_copies(copies_ref, masked_sums(second_ref, mask_ref))


def plain_body(
    total_ref, pre_ref, mask_ref, count_ref, gain_ref, bias_ref, spatial_ref,
    wide_ref, second_ref, copies_ref, stats_ref,
    padded_ref, shifted_ref,
):
    pixels, width = pre_ref.shape
    side = 1 << ((pixels.bit_length() - 1) // 2)
    total = read_copies(total_ref)
    mean, var = moments(total, width, count_ref[0:1, 0:1])
    stats_ref[...] = jnp.concatenate([mean, var], axis=0)
    scale, shift = scale_shift(mean, var, gain_ref[:, :width], bias_ref[:, :width])
    padded_ref[...] = jnp.zeros_like(padded_ref)
    activate(pre_ref, mask_ref, scale, shift, padded_ref, 2 * side)
    wide_ref[...] = padded_ref[pl.ds(2 * side, pixels), :]
    flush(wide_ref)
    build_taps(padded_ref, shifted_ref, pixels, side)
    need(spatial_ref)
    second_ref[...] = jnp.zeros_like(second_ref)
    for tap_index in range(9):
        taps = tap_of(shifted_ref, tap_index, pixels, side)
        second_ref[...] = second_ref[...] + dot_nn(taps, spatial_ref[tap_index])
    write_copies(copies_ref, masked_sums(second_ref, mask_ref))


def third_body(
    total_ref, pre_ref, mask_ref, count_ref, gain_ref, bias_ref, expand_ref,
    act_ref, wide_ref, third_ref, copies_ref, stats_ref,
):
    pixels, width = pre_ref.shape
    channels = third_ref.shape[1]
    total = read_copies(total_ref)
    mean, var = moments(total, width, count_ref[0:1, 0:1])
    stats_ref[...] = jnp.concatenate([mean, var], axis=0)
    scale, shift = scale_shift(
        mean, var, gain_ref[:, width : 2 * width], bias_ref[:, width : 2 * width]
    )
    activate(pre_ref, mask_ref, scale, shift, act_ref)
    wide_ref[...] = act_ref[...].astype(f32)
    flush(act_ref)
    flush(wide_ref)
    need(expand_ref)
    sums, squares = ([], [])
    for start, size in spans_of(channels, 256):
        block = dot_nn(act_ref[...], expand_ref[:, start : start + size])
        third_ref[:, start : start + size] = block
        sums.append(jnp.sum(block, axis=0, keepdims=True))
        squares.append(jnp.sum(block * block, axis=0, keepdims=True))
    flush(third_ref)
    write_copies(copies_ref, sums + squares)


def between_body(
    total_ref, pre_ref, images_ref, mask_ref, count_ref, place_ref, gain_ref, bias_ref, squeeze_ref,
    summed_ref, low_ref, half_ref, first_ref, copies_ref, stats_ref,
):
    pixels, channels = pre_ref.shape
    total = read_copies(total_ref)
    mean, var = moments(total, channels, count_ref[0:1, 0:1])
    stats_ref[...] = jnp.concatenate([mean, var], axis=0)
    begin = gain_ref.shape[1] - channels
    scale, shift = scale_shift(mean, var, gain_ref[:, begin:], bias_ref[:, begin:])
    for start, size in spans_of(channels, 512):
        span = pl.ds(start, size)

        def step(rows, carry):
            summed = (
                pre_ref[rows, span] * scale[:, start : start + size]
                + shift[:, start : start + size]
                + images_ref[rows, span].astype(f32)
            )
            summed_ref[rows, span] = summed
            low_ref[rows, span] = (silu(summed) * wide_mask(mask_ref, rows, size)).astype(bf16)
            return carry

        row_loop(pixels, step, 0)
    flush(summed_ref)
    flush(low_ref)
    need(squeeze_ref)
    sums, squares = ([], [])
    for start, size in spans_of(first_ref.shape[1], 256):
        block = dot_nn(low_ref[...], squeeze_ref[:, start : start + size])
        first_ref[:, start : start + size] = block
        sums.append(jnp.sum(block, axis=0, keepdims=True))
        squares.append(jnp.sum(block * block, axis=0, keepdims=True))
    write_copies(copies_ref, sums + squares)
    half = half_ref.shape[1]
    other = pl.multiple_of((1 - place_ref[0, 0]) * half, lane)
    half_ref[...] = low_ref[:, pl.ds(other, half)].astype(f32)


def turn_body(
    total_ref, pre_ref, before_ref, grad_ref, mask_ref, count_ref, gain_ref, bias_ref,
    image_ref, grad_sum_ref, copies_ref, stats_ref,
):
    pixels, channels = pre_ref.shape
    total = read_copies(total_ref)
    mean, var = moments(total, channels, count_ref[0:1, 0:1])
    stats_ref[...] = jnp.concatenate([mean, var], axis=0)
    begin = gain_ref.shape[1] - channels
    scale, shift = scale_shift(mean, var, gain_ref[:, begin:], bias_ref[:, begin:])
    inverse = lax.rsqrt(var + eps_norm)
    sums, prods = ([], [])
    for start, size in spans_of(channels, 512):
        span = pl.ds(start, size)
        cut = slice(start, start + size)

        def both(rows):
            mask = wide_mask(mask_ref, rows, size)
            pre = pre_ref[rows, span]
            summed = pre * scale[:, cut] + shift[:, cut] + silu(before_ref[rows, span]) * mask
            gate = logistic(summed)
            image_ref[rows, span] = (summed * gate * mask).astype(bf16)
            slope = gate * (1.0 + summed * (1.0 - gate))
            grad = grad_ref[rows, span].astype(f32) * mask * slope
            grad_sum_ref[rows, span] = grad
            return (grad, grad * ((pre - mean[:, cut]) * inverse[:, cut]))

        total_grad, total_prod = two_sums(pixels, size, both)
        sums.append(total_grad)
        prods.append(total_prod)
    flush(image_ref)
    flush(grad_sum_ref)
    write_copies(copies_ref, sums + prods)


def low_gradient(rows, width, start, grad, pre, mask, coefs):
    cut = slice(start, start + width)
    scale, mean_grad, mean_prod, mean = (part[:, cut] for part in coefs[:4])
    return scale * (grad - mask * (mean_grad + (pre - mean) * mean_prod))


def back_third_body(
    total_ref, grad_sum_ref, pre_ref, stats_ref, second_ref, second_stats_ref, mask_ref, count_ref,
    place_ref, gain_ref, bias_ref, expand_ref,
    low_ref, half_ref, grad_ref, copies_ref, result_ref,
):
    pixels, channels = pre_ref.shape
    width = second_ref.shape[1]
    total = read_copies(total_ref)
    coefs = grad_rows(
        total, stats_ref[...], gain_ref[:, 2 * width :], count_ref[0:1, 0:1], channels
    )
    result_ref[...] = jnp.concatenate(coefs[4:6], axis=0)
    for start, size in spans_of(channels, 512):
        span = pl.ds(start, size)

        def step(rows, carry):
            mask = wide_mask(mask_ref, rows, size)
            low_ref[rows, span] = low_gradient(
                rows, size, start, grad_sum_ref[rows, span], pre_ref[rows, span], mask, coefs
            ).astype(bf16)
            return carry

        row_loop(pixels, step, 0)
    half = half_ref.shape[1]
    other = pl.multiple_of((1 - place_ref[0, 0]) * half, lane)
    half_ref[...] = low_ref[:, pl.ds(other, half)].astype(f32)
    flush(low_ref)
    flush(half_ref)
    for ref in (expand_ref, second_ref, second_stats_ref):
        need(ref)
    for start, size in spans_of(width, 256):
        grad_ref[:, start : start + size] = dot_nt(low_ref[...], expand_ref[start : start + size, :])
    norm_two_slope(grad_ref, second_ref, second_stats_ref, mask_ref, gain_ref, bias_ref, width, copies_ref)


def norm_two_slope(grad_ref, pre_ref, stats_ref, mask_ref, gain_ref, bias_ref, begin, copies_ref):
    pixels, width = pre_ref.shape
    mean, var = (stats_ref[0:1, :], stats_ref[1:2, :])
    inverse = lax.rsqrt(var + eps_norm)
    scale, shift = scale_shift(
        mean, var, gain_ref[:, begin : begin + width], bias_ref[:, begin : begin + width]
    )

    def both(rows):
        pre = pre_ref[rows, :]
        slope = silu_slope(pre * scale + shift)
        grad = grad_ref[rows, :] * slope * wide_mask(mask_ref, rows, width)
        grad_ref[rows, :] = grad
        return (grad, grad * ((pre - mean) * inverse))

    write_copies(copies_ref, two_sums(pixels, width, both))


def low_second(total_ref, grad_ref, pre_ref, stats_ref, mask_ref, count_ref, gain, low_ref, result_ref):
    pixels, width = pre_ref.shape
    total = read_copies(total_ref)
    coefs = grad_rows(total, stats_ref[...], gain, count_ref[0:1, 0:1], width)
    result_ref[...] = jnp.concatenate(coefs[4:6], axis=0)

    def step(rows, carry):
        mask = wide_mask(mask_ref, rows, width)
        low_ref[rows, :] = low_gradient(
            rows, width, 0, grad_ref[rows, :], pre_ref[rows, :], mask, coefs
        ).astype(bf16)
        return carry

    row_loop(pixels, step, 0)


def back_plain_body(
    total_ref, grad_in_ref, second_ref, second_stats_ref, first_ref, first_stats_ref, mask_ref,
    count_ref, place_ref, gain_ref, bias_ref, spatial_ref,
    low_ref, half_ref, grad_ref, copies_ref, result_ref,
    sums_ref,
):
    pixels, width = second_ref.shape
    side = 1 << ((pixels.bit_length() - 1) // 2)
    low_second(
        total_ref, grad_in_ref, second_ref, second_stats_ref, mask_ref, count_ref,
        gain_ref[:, width : 2 * width], low_ref, result_ref,
    )
    half = half_ref.shape[1]
    other = pl.multiple_of((1 - place_ref[0, 0]) * half, lane)
    half_ref[...] = low_ref[:, pl.ds(other, half)].astype(f32)
    flush(low_ref)
    flush(half_ref)
    need(spatial_ref)
    sums_ref[...] = jnp.zeros_like(sums_ref)
    for tap_index in range(9):
        tap_rows_out(
            sums_ref, tap_index, pixels, side, dot_nt(low_ref[...], spatial_ref[tap_index])
        )
    grad_ref[...] = fold_columns(sums_ref, pixels, side)
    norm_two_slope(grad_ref, first_ref, first_stats_ref, mask_ref, gain_ref, bias_ref, 0, copies_ref)


def back_deform_body(
    total_ref, grad_in_ref, second_ref, second_stats_ref, first_ref, first_stats_ref, mask_ref,
    count_ref, place_ref, gain_ref, bias_ref, spatial_ref, act_ref, offsets_ref, weights_ref,
    low_ref, half_ref, grad_ref, copies_ref, result_ref, grad_offsets_ref,
    sums_ref, padded_ref, shifted_ref,
):
    pixels, width = second_ref.shape
    side = 1 << ((pixels.bit_length() - 1) // 2)
    low_second(
        total_ref, grad_in_ref, second_ref, second_stats_ref, mask_ref, count_ref,
        gain_ref[:, width : 2 * width], low_ref, result_ref,
    )
    half = half_ref.shape[1]
    other = pl.multiple_of((1 - place_ref[0, 0]) * half, lane)
    half_ref[...] = low_ref[:, pl.ds(other, half)].astype(f32)
    flush(low_ref)
    flush(half_ref)
    for ref in (first_ref, first_stats_ref, spatial_ref, act_ref, offsets_ref, weights_ref):
        need(ref)
    offsets = offsets_ref[...]
    outs = offsets.shape[1]
    channel = lax.broadcasted_iota(jnp.int32, (pixels, outs), 1)
    moved = jnp.zeros((pixels, outs), f32)
    grad_ref[...] = jnp.zeros_like(grad_ref)
    for tap_index in range(9):
        dist_y, dist_x, bump_y, bump_x = tap_factors(offsets, tap_index, side)
        weight_y, weight_x = (bump_y * bump_y, bump_x * bump_x)
        sampling = (weight_y * weight_x).astype(bf16)
        piece = dot_nt(low_ref[...], spatial_ref[tap_index]).astype(bf16)
        grad_ref[...] = grad_ref[...] + dot_tn(sampling, piece)
        product = -4.0 * dot_nt(piece, act_ref[...])
        along_y = jnp.sum(product * (dist_y * bump_y * weight_x), axis=1, keepdims=True)
        along_x = jnp.sum(product * (dist_x * bump_x * weight_y), axis=1, keepdims=True)
        moved = moved + jnp.where(channel == 2 * tap_index, along_y, 0.0)
        moved = moved + jnp.where(channel == 2 * tap_index + 1, along_x, 0.0)
    moved_low = moved.astype(bf16)
    padded_ref[...] = jnp.zeros_like(padded_ref)
    padded_ref[pl.ds(2 * side, pixels), :] = act_ref[...].astype(f32)
    build_taps(padded_ref, shifted_ref, pixels, side)
    sums_ref[...] = jnp.zeros_like(sums_ref)
    grad_offsets_ref[...] = jnp.zeros_like(grad_offsets_ref)
    for tap_index in range(9):
        taps = tap_of(shifted_ref, tap_index, pixels, side)
        first = tap_index * outs
        grad_offsets_ref[first : first + outs, :] = dot_tn(moved_low, taps)
        tap_rows_out(
            sums_ref, tap_index, pixels, side, dot_nt(moved_low, weights_ref[tap_index])
        )
    grad_ref[...] = grad_ref[...] + fold_columns(sums_ref, pixels, side)
    norm_two_slope(grad_ref, first_ref, first_stats_ref, mask_ref, gain_ref, bias_ref, 0, copies_ref)


def back_between_body(
    total_ref, grad_ref, first_ref, first_stats_ref, grad_sum_ref, summed_ref, pre_ref, stats_ref,
    mask_ref, count_ref, gain_ref, squeeze_ref,
    low_ref, wide_ref, next_ref, copies_ref, result_ref,
):
    pixels, width = first_ref.shape
    channels = pre_ref.shape[1]
    low_second(
        total_ref, grad_ref, first_ref, first_stats_ref, mask_ref, count_ref,
        gain_ref[:, :width], low_ref, result_ref,
    )
    wide_ref[...] = low_ref[...].astype(f32)
    flush(low_ref)
    flush(wide_ref)
    for ref in (grad_sum_ref, summed_ref, pre_ref, stats_ref, squeeze_ref):
        need(ref)
    mean, var = (stats_ref[0:1, :], stats_ref[1:2, :])
    inverse = lax.rsqrt(var + eps_norm)
    sums, prods = ([], [])
    for start, size in spans_of(channels, 512):
        span = pl.ds(start, size)
        cut = slice(start, start + size)
        next_ref[:, span] = dot_nt(low_ref[...], squeeze_ref[start : start + size, :])

        def both(rows):
            mask = wide_mask(mask_ref, rows, size)
            slope = silu_slope(summed_ref[rows, span])
            grad = (next_ref[rows, span] + grad_sum_ref[rows, span]) * mask * slope
            next_ref[rows, span] = grad
            return (grad, grad * ((pre_ref[rows, span] - mean[:, cut]) * inverse[:, cut]))

        total_grad, total_prod = two_sums(pixels, size, both)
        sums.append(total_grad)
        prods.append(total_prod)
    write_copies(copies_ref, sums + prods)


def last_low_body(
    total_ref, grad_ref, first_ref, first_stats_ref, mask_ref, count_ref, gain_ref,
    low_ref, wide_ref, result_ref,
):
    width = first_ref.shape[1]
    low_second(
        total_ref, grad_ref, first_ref, first_stats_ref, mask_ref, count_ref,
        gain_ref[:, :width], low_ref, result_ref,
    )
    wide_ref[...] = low_ref[...].astype(f32)


def last_body(low_ref, grad_sum_ref, squeeze_ref, image_ref, token_ref):
    token_ref[...] = jnp.zeros_like(token_ref)
    for start, size in spans_of(image_ref.shape[1], 256):
        block = dot_nt(low_ref[...], squeeze_ref[start : start + size, :])
        image_ref[:, start : start + size] = (
            block + grad_sum_ref[:, start : start + size]
        ).astype(bf16)


def sum_copies_body(copies_ref, out_ref):
    total = jnp.sum(copies_ref[...], axis=0)

    def one_copy(step, carry):
        out_ref[step] = total
        return carry

    lax.fori_loop(0, out_ref.shape[0], one_copy, 0)


block_cols = 256


def split_chunks(scratch_ref, keep_ref, send_ref, own, place, spot):
    for index in range(keep_ref.shape[0]):
        low = index & ((1 << place) - 1)
        base = ((index >> place) << (place + 1)) | low
        keep_ref[index, spot] = scratch_ref[base + own * (1 << place)]
        send_ref[index, spot] = scratch_ref[base + (1 - own) * (1 << place)]


def weights_body(kinds, firsts, spans, own_place_ref, *refs):
    groups = [refs[4 * place : 4 * place + 4] for place in range(len(kinds))]
    rest = refs[4 * len(kinds) :]
    streams = len(spans)
    outs, token_ref = (rest[: 2 * streams], rest[2 * streams])
    chunks_ref, scratch = (rest[2 * streams + 1], list(rest[2 * streams + 2 :]))
    token_ref[...] = jnp.zeros_like(token_ref)
    count, depth, _ = chunks_ref.shape
    makers = []
    for kind, (rows_ref, rows_other_ref, cols_ref, cols_other_ref) in zip(kinds, groups):
        for ref in (rows_ref, rows_other_ref, cols_ref, cols_other_ref):
            need(ref)
        pixels, half = cols_other_ref.shape
        side = 1 << ((pixels.bit_length() - 1) // 2)
        both_cols = scratch.pop(0)
        start_own = pl.multiple_of(own_place_ref[0, 0] * half, lane)
        both_cols[pl.ds(0, pixels), :] = cols_ref[:, pl.ds(start_own, half)]
        both_cols[pl.ds(pixels, pixels), :] = cols_other_ref[...].astype(bf16)
        if kind == "rows":
            both_rows = scratch.pop(0)
            both_rows[pl.ds(0, pixels), :] = rows_ref[...]
            both_rows[pl.ds(pixels, pixels), :] = rows_other_ref[...].astype(bf16)
            for start in range(0, half, block_cols):
                makers.append(
                    lambda rows=both_rows, cols=both_cols, start=start: dot_tn(
                        rows[...], cols[:, start : start + block_cols]
                    )
                )
        elif kind == "plain":
            padded, taps = (scratch.pop(0), (scratch.pop(0), scratch.pop(0)))
            for source, shifted in zip((rows_ref, rows_other_ref), taps):
                padded[...] = jnp.zeros_like(padded)
                padded[pl.ds(2 * side, pixels), :] = source[...]
                build_taps(padded, shifted, pixels, side)
            for tap in range(9):
                makers.append(
                    lambda taps=taps, cols=both_cols, tap=tap, pixels=pixels, side=side: dot_tn(
                        tap_of(taps[0], tap, pixels, side), cols[pl.ds(0, pixels), :]
                    )
                    + dot_tn(tap_of(taps[1], tap, pixels, side), cols[pl.ds(pixels, pixels), :])
                )
        else:
            width = cols_ref.shape[1]
            for tap in range(9):
                span = slice(tap * width, (tap + 1) * width)
                makers.append(
                    lambda one=rows_ref, two=rows_other_ref, cols=both_cols, span=span, pixels=pixels: dot_tn(
                        one[:, span], cols[pl.ds(0, pixels), :]
                    )
                    + dot_tn(two[:, span].astype(bf16), cols[pl.ds(pixels, pixels), :])
                )
    for stream, (start, stop) in enumerate(spans):
        bit = firsts[stream]
        own = own_place_ref[0, bit]
        for part in range(start, stop):
            chunks_ref[...] = makers[part]().reshape(count, depth, block_cols)
            split_chunks(
                chunks_ref, outs[2 * stream], outs[2 * stream + 1], own, bit - 1, part - start
            )
        flush(outs[2 * stream + 1])
        flush(outs[2 * stream])


def step_body(spots, own_place_ref, *refs):
    streams = len(spots)
    kept, came = (refs[:streams], refs[streams : 2 * streams])
    outs = refs[2 * streams :]
    outs[-1][...] = jnp.zeros_like(outs[-1])
    for stream, (bit, place) in enumerate(spots):
        own = own_place_ref[0, bit]
        need(kept[stream])
        need(came[stream])
        keep_ref, send_ref = (outs[2 * stream], outs[2 * stream + 1])
        for index in range(keep_ref.shape[0]):
            low = index & ((1 << place) - 1)
            base = ((index >> place) << (place + 1)) | low
            theirs = base + (1 - own) * (1 << place)
            send_ref[index] = kept[stream][theirs] + came[stream][theirs]
        flush(send_ref)
        for index in range(keep_ref.shape[0]):
            low = index & ((1 << place) - 1)
            base = ((index >> place) << (place + 1)) | low
            mine = base + own * (1 << place)
            keep_ref[index] = kept[stream][mine] + came[stream][mine]
        flush(keep_ref)


def last_step_body(streams, *refs):
    kept, came, out_ref = (refs[:streams], refs[streams : 2 * streams], refs[2 * streams])
    refs[-1][...] = jnp.zeros_like(refs[-1])
    start = 0
    for stream in range(streams):
        stop = start + kept[stream].shape[1]
        out_ref[start:stop] = kept[stream][0] + came[stream][0]
        start = stop


def assemble_body(kinds, flips, own_place_ref, own_ref, pair_ref, side_ref, both_ref, *outs):
    outs[-1 - sum(flips)][...] = jnp.zeros_like(outs[-1 - sum(flips)])
    turned = list(outs[len(outs) - sum(flips) :])
    rows, cols = own_ref.shape[-2:]
    pair, line = (own_place_ref[0, 0], own_place_ref[0, 1])
    for row_at, col_at in ((0, 0), (0, 1), (1, 0), (1, 1)):
        same_row, same_col = (line == row_at, pair == col_at)
        row_span = slice(row_at * rows, (row_at + 1) * rows)

        def chosen(part):
            near = jnp.where(same_col, own_ref[part], pair_ref[part])
            far = jnp.where(same_col, side_ref[part], both_ref[part])
            return jnp.where(same_row, near, far)

        part = 0
        used = 0
        for place, kind in enumerate(kinds):
            if kind == "rows":
                target = outs[place]
                if flips[place]:
                    target = turned[used]
                    used += 1
                parts = target.shape[1] // 2 // cols
                for step in range(parts):
                    at = (col_at * parts + step) * cols
                    target[row_span, at : at + cols] = chosen(part + step)
                part += parts
            else:
                for step in range(9):
                    outs[place][step, row_span, col_at * cols : (col_at + 1) * cols] = chosen(part + step)
                part += 9
    used = 0
    for place, flip in enumerate(flips):
        if flip:
            width = turned[used].shape[1]
            for start in range(0, width, block_cols):
                outs[place][start : start + block_cols, :] = turned[used][:, start : start + block_cols].T
            used += 1


class Comm:
    def __init__(self, wide_size, narrow_size):
        self.total = wide_size * narrow_size
        self.bits = self.total.bit_length() - 1
        self.low = narrow_size.bit_length() - 1
        self.index = lax.axis_index("wide") * narrow_size + lax.axis_index("narrow")
        self.places = jnp.stack([self.bit(place) for place in range(self.bits)])[None, :]

    def bit(self, place):
        return (self.index >> place) & 1

    def swap_over(self, values, flips):
        pairs = [(source, source ^ flips) for source in range(self.total)]
        return lax.ppermute(values, axes, pairs)

    def swap(self, values, place):
        return self.swap_over(values, 1 << place)

    def sync(self, copies):
        return lax.all_to_all(copies, axes, 0, 0, tiled=True)

    def orders(self):
        outer = list(range(self.low, self.bits))
        inner = list(range(1, self.low))
        return (
            outer[:1] + inner + outer[1:],
            inner + outer[1:2] + outer[:1] + outer[2:],
            outer[1:2] + outer[:1] + inner + outer[2:],
        )


token = (8, lane)


class Chain:
    def __init__(self, comm, kinds, groups, after=()):
        self.comm = comm
        self.kinds = kinds
        self.orders = comm.orders()
        pixels, rows = groups[0][0].shape
        if kinds[0] == "given":
            rows = groups[0][2].shape[1]
        self.rows = rows
        chunks = 1 << (comm.bits - 1)
        depth = rows // chunks
        side = 1 << ((pixels.bit_length() - 1) // 2)
        total = 0
        scratch = [pltpu.VMEM((chunks, depth, block_cols), f32)]
        self.shapes = []
        for kind, (_, _, cols_op, cols_other) in zip(kinds, groups):
            half = cols_other.shape[1]
            scratch.append(pltpu.VMEM((2 * pixels, half), bf16))
            if kind == "rows":
                total += half // block_cols
                scratch.append(pltpu.VMEM((2 * pixels, rows), bf16))
                self.shapes.append((2 * depth, 2 * half))
            else:
                total += 9
                self.shapes.append((9, 2 * depth, 2 * half))
            if kind == "plain":
                scratch.append(pltpu.VMEM((pixels + 4 * side, rows), f32))
                scratch += [pltpu.VMEM((3, pixels + 4 * side, rows), bf16)] * 2
        first = -(-total // 3)
        second = first + -(-(total - first) // 2)
        spans = ((0, first), (first, second), (second, total))
        outs = []
        for start, stop in spans:
            outs += [shape_of((chunks // 2, stop - start, depth, block_cols))] * 2
        args = (comm.places,) + tuple(part for group in groups for part in group)
        pieces = call(
            functools.partial(weights_body, kinds, tuple(order[0] for order in self.orders), spans),
            outs + [shape_of(token)], args, (0,), scratch, after, tuple(range(1, len(args))),
        )
        self.left = [
            [place for place in range(1, comm.bits) if place != order[0]] for order in self.orders
        ]
        self.at = 0
        self.quarters = []
        self.token = pieces[-1]
        self.exchange(pieces)

    def exchange(self, pieces):
        self.kept = pieces[0:-1:2]
        self.came = [
            self.comm.swap(sent, order[self.at]) for sent, order in zip(pieces[1:-1:2], self.orders)
        ]
        self.at += 1

    def step(self, after=()):
        count = len(self.kept)
        if self.at < len(self.orders[0]):
            spots, outs = ([], [])
            for stream, order in enumerate(self.orders):
                bit = order[self.at]
                spots.append((bit, self.left[stream].index(bit)))
                self.left[stream].remove(bit)
                shape = self.kept[stream].shape
                outs += [shape_of((shape[0] // 2,) + shape[1:])] * 2
            pieces = call(
                functools.partial(step_body, tuple(spots)),
                outs + [shape_of(token)],
                (self.comm.places, *self.kept, *self.came), (0,), (), after,
                tuple(range(1, 1 + 2 * count)),
            )
            self.token = pieces[-1]
            self.exchange(pieces)
        else:
            shape = list(self.kept[0].shape[1:])
            shape[0] = sum(piece.shape[1] for piece in self.kept)
            joined, self.token = call(
                functools.partial(last_step_body, count),
                [shape_of(tuple(shape)), shape_of(token)],
                (*self.kept, *self.came), (), (), after,
            )
            self.quarters = [joined] + [self.comm.swap_over(joined, flips) for flips in (1, 2, 3)]
        return self

    def finish(self, flips, after=()):
        while not self.quarters:
            self.step(after)
        outs = [shape_of(shape[::-1] if flip else shape) for shape, flip in zip(self.shapes, flips)]
        scratch = [pltpu.VMEM(shape, f32) for shape, flip in zip(self.shapes, flips) if flip]
        *results, self.token = call(
            functools.partial(assemble_body, self.kinds, flips),
            outs + [shape_of(token)], (self.comm.places, *self.quarters), (0,), scratch, after,
        )
        return results


def per_device(
    wide_size, narrow_size, images, image_sizes, offset_shift, squeeze_one, offsets_one, spatial_one,
    expand_one, squeeze_two, spatial_two, expand_two, norm_gain_one, norm_bias_one, norm_gain_two,
    norm_bias_two, run_mean_one, run_var_one, run_mean_two, run_var_two, grad_output,
):
    comm = Comm(wide_size, narrow_size)
    side, channels = (images.shape[1], images.shape[3])
    pixels = side * side
    width = squeeze_one.shape[1]
    outs = offsets_one.shape[2]
    total = comm.total
    small = (total, 2 * width // lane, lane)
    large = (total, 2 * channels // lane, lane)
    flat = images.reshape(pixels, channels)
    grad_out = grad_output.reshape(pixels, channels)
    gain_one, bias_one = (norm_gain_one[None, :], norm_bias_one[None, :])
    gain_two, bias_two = (norm_gain_two[None, :], norm_bias_two[None, :])
    field = shape_of((pixels, width))
    field_low = shape_of((pixels, width), bf16)
    plane = shape_of((pixels, channels))
    plane_low = shape_of((pixels, channels), bf16)
    half_plane = shape_of((pixels, channels // 2))
    half_field = shape_of((pixels, width // 2))
    stats_small, stats_large = (shape_of((2, width)), shape_of((2, channels)))
    padded = pltpu.VMEM((pixels + 4 * side, width), f32)
    shifted = pltpu.VMEM((3, pixels + 4 * side, width), bf16)
    tap_sums = pltpu.VMEM((3, pixels + 4 * side, width), f32)

    first_one, mask, copies, images_half = call(
        first_body,
        (field, shape_of((pixels, lane)), shape_of((total, 2 * width // lane + 8, lane)), half_plane),
        (image_sizes, comm.places, flat, squeeze_one),
        (0, 1),
    )
    images_half = comm.swap(images_half, 0)
    copies = comm.sync(copies)
    (act_one, columns, columns_wide, offsets, second_one, copies, first_stats_one, count) = call(
        deform_body,
        (
            field_low, shape_of((pixels, 9 * width), bf16), shape_of((pixels, 9 * width)),
            shape_of((pixels, outs)), field, shape_of(small), stats_small, shape_of((8, lane)),
        ),
        (
            copies, first_one, mask, gain_one, bias_one, offsets_one,
            offset_shift.astype(f32)[None, :], spatial_one,
        ),
        (),
        (padded, shifted),
        (),
        (5, 7),
    )
    columns_wide = comm.swap(columns_wide, 0)
    copies = comm.sync(copies)
    act_second_one, act_second_wide_one, third_one, copies, second_stats_one = call(
        third_body,
        (field_low, field, plane, shape_of(large), stats_small),
        (copies, second_one, mask, count, gain_one, bias_one, expand_one), late=(6,),
    )
    act_second_wide_one = comm.swap(act_second_wide_one, 0)
    copies = comm.sync(copies)
    summed_one, low_two, low_half, first_two, copies, third_stats_one = call(
        between_body,
        (plane, plane_low, half_plane, field, shape_of(small), stats_large),
        (copies, third_one, flat, mask, count, comm.places, gain_one, bias_one, squeeze_two),
        (5,), late=(8,),
    )
    low_half = comm.swap(low_half, 0)
    copies = comm.sync(copies)
    act_wide_two, second_two, copies, first_stats_two = call(
        plain_body,
        (field, field, shape_of(small), stats_small),
        (copies, first_two, mask, count, gain_two, bias_two, spatial_two),
        (),
        (padded, shifted), late=(6,),
    )
    act_wide_two_other = comm.swap(act_wide_two, 0)
    copies = comm.sync(copies)
    act_second_two, act_second_wide_two, third_two, copies, second_stats_two = call(
        third_body,
        (field_low, field, plane, shape_of(large), stats_small),
        (copies, second_two, mask, count, gain_two, bias_two, expand_two), late=(6,),
    )
    act_second_wide_two = comm.swap(act_second_wide_two, 0)
    copies = comm.sync(copies)
    output_images, grad_sum_two, copies, third_stats_two = call(
        turn_body,
        (plane_low, plane, shape_of(large), stats_large),
        (copies, third_two, summed_one, grad_out, mask, count, gain_two, bias_two),
    )
    copies = comm.sync(copies)
    low_third_two, third_half, grad_second_two, copies, third_result_two = call(
        back_third_body,
        (plane_low, half_plane, field, shape_of(small), stats_large),
        (
            copies, grad_sum_two, third_two, third_stats_two, second_two, second_stats_two, mask, count,
            comm.places, gain_two, bias_two, expand_two,
        ),
        (8,), late=(4, 5, 11),
    )
    third_half = comm.swap(third_half, 0)
    copies = comm.sync(copies)
    low_second_two, second_half, grad_first_two, copies, second_result_two = call(
        back_plain_body,
        (field_low, half_field, field, shape_of(small), stats_small),
        (
            copies, grad_second_two, second_two, second_stats_two, first_two, first_stats_two, mask,
            count, comm.places, gain_two, bias_two, spatial_two,
        ),
        (8,),
        (tap_sums,),
        (),
        (11,),
    )
    second_half = comm.swap(second_half, 0)
    copies = comm.sync(copies)
    chain_one = Chain(
        comm, ("rows", "plain"),
        (
            (act_second_two, act_second_wide_two, low_third_two, third_half),
            (act_wide_two, act_wide_two_other, low_second_two, second_half),
        ),
    )
    low_first_two, low_first_wide, grad_sum_one, copies, first_result_two = call(
        back_between_body,
        (field_low, field, plane, shape_of(large), stats_small),
        (
            copies, grad_first_two, first_two, first_stats_two, grad_sum_two, summed_one, third_one,
            third_stats_one, mask, count, gain_two, squeeze_two,
        ),
        (),
        (),
        (chain_one.token,),
        (4, 5, 6, 7, 11),
    )
    low_first_wide = comm.swap(low_first_wide, 0)
    copies = comm.sync(copies)
    low_third_one, third_half, grad_second_one, copies, third_result_one = call(
        back_third_body,
        (plane_low, half_plane, field, shape_of(small), stats_large),
        (
            copies, grad_sum_one, third_one, third_stats_one, second_one, second_stats_one, mask, count,
            comm.places, gain_one, bias_one, expand_one,
        ),
        (8,),
        (),
        (),
        (4, 5, 11),
    )
    third_half = comm.swap(third_half, 0)
    copies = comm.sync(copies)
    chain_one.step((third_result_one,))
    slots = -(-9 * outs // total)
    slots = -(-slots // 8) * 8
    low_second_one, second_half, grad_first_one, copies, second_result_one, grad_offsets = call(
        back_deform_body,
        (
            field_low, half_field, field, shape_of(small), stats_small, shape_of((total * slots, width)),
        ),
        (
            copies, grad_second_one, second_one, second_stats_one, first_one, first_stats_one, mask,
            count, comm.places, gain_one, bias_one, spatial_one, act_one, offsets, offsets_one,
        ),
        (8,),
        (tap_sums, padded, shifted),
        (chain_one.token,),
        (4, 5, 11, 12, 13, 14),
    )
    second_half = comm.swap(second_half, 0)
    copies = comm.sync(copies)
    chain_one.step((second_result_one,))
    chain_two = Chain(
        comm, ("rows", "rows", "given"),
        (
            (low_first_two, low_first_wide, low_two, low_half),
            (act_second_one, act_second_wide_one, low_third_one, third_half),
            (columns, columns_wide, low_second_one, second_half),
        ),
        (chain_one.token,),
    )
    low_first_one, low_first_wide, first_result_one = call(
        last_low_body,
        (field_low, field, stats_small),
        (copies, grad_first_one, first_one, first_stats_one, mask, count, gain_one),
        (),
        (),
        (chain_two.token,),
    )
    low_first_wide = comm.swap(low_first_wide, 0)
    grad_offsets = comm.sync(grad_offsets.reshape(total, slots, width))
    grad_images, last_token = call(
        last_body,
        (plane_low, shape_of(token)),
        (low_first_one, grad_sum_one, squeeze_one),
    )
    chain_three = Chain(
        comm, ("rows",), ((low_first_one, low_first_wide, flat, images_half),), (last_token,)
    )
    (grad_offsets,) = call(
        sum_copies_body, (shape_of((total, slots, width)),), (grad_offsets,), (), (),
        (chain_three.token,),
    )
    grad_offsets = comm.sync(grad_offsets)
    last = chain_three.token
    for chain in (
        chain_one, chain_one, chain_three, chain_two, chain_three, chain_two, chain_three, chain_two,
        chain_three, chain_two,
    ):
        last = chain.step((last,)).token
    grad_expand_two, grad_spatial_two = chain_one.finish((False, False), (last,))
    (grad_squeeze_one,) = chain_three.finish((True,), (last,))
    grad_squeeze_two, grad_expand_one, grad_spatial_one = chain_two.finish((True, False, False), (last,))

    def laid(parts, row):
        return jnp.concatenate([part[row] for part in parts])

    results_one = (first_result_one, second_result_one, third_result_one)
    results_two = (first_result_two, second_result_two, third_result_two)
    stats_one = (first_stats_one, second_stats_one, third_stats_one)
    stats_two = (first_stats_two, second_stats_two, third_stats_two)
    pixel_count = count[0, 0]
    unbias = pixel_count / (pixel_count - 1.0)
    fresh = 1.0 - keep_rate
    return (
        output_images.reshape(images.shape),
        grad_images.reshape(images.shape),
        grad_squeeze_one,
        grad_offsets.reshape(total * slots, width)[: 9 * outs].reshape(9, outs, width).transpose(0, 2, 1),
        grad_spatial_one,
        grad_expand_one,
        grad_squeeze_two,
        grad_spatial_two,
        grad_expand_two,
        laid(results_one, 1),
        laid(results_one, 0),
        laid(results_two, 1),
        laid(results_two, 0),
        keep_rate * run_mean_one + fresh * laid(stats_one, 0),
        keep_rate * run_var_one + fresh * laid(stats_one, 1) * unbias,
        keep_rate * run_mean_two + fresh * laid(stats_two, 0),
        keep_rate * run_var_two + fresh * laid(stats_two, 1) * unbias,
    )


def solution(mesh):
    images_spec = P(axes, None, None, None)
    whole = P()
    return jax.shard_map(
        functools.partial(per_device, mesh.shape["wide"], mesh.shape["narrow"]),
        mesh=mesh,
        in_specs=(images_spec, P(axes, None)) + (whole,) * 16 + (images_spec,),
        out_specs=(
            images_spec,
            images_spec,
            P(None, "wide"),
            whole,
            P(None, "wide", None),
            P("wide", None),
            P(None, "wide"),
            P(None, "wide", None),
            P("wide", None),
        )
        + (whole,) * 8,
        check_vma=False,
    )
```

time: 1270 us -> 578 us (0.46)
  blocking collectives: 493 us -> 94.6 us
  waiting for transfers between devices: 485 us -> 201 us
  Pallas kernels: 0 us -> 165 us
  matrix products: 99.7 us -> 0 us
  starting transfers between devices: 0.33 us -> 75.8 us
  other arithmetic: 77.1 us -> 2.97 us
  local copies, waits for them, and re-layouts: 81.8 us -> 26.1 us
  between operations: 20.6 us -> 3.44 us
    psum x12 -> x0, blocking collectives: 493 us -> none  [the longest x5 208 us: norm_backward(): lax.psum((jnp.sum(grad_norm, axis=0), jnp.sum(grad_norm * normed, axis=0)...]
    reduce_scatter x6 -> x0, waiting for transfers between devices: 403 us -> none  [the longest x2 337 us: sum_gradients(): lax.psum_scatter(grad_spatial, 'wide', scatter_dimension=1, tiled=True)]
    pallas_call x0 -> x33, Pallas kernels: none -> 165 us  [call(): pl.pallas_call(kernel, out_shape=tuple(outs), in_specs=specs, out_specs=t...]
    ppermute x0 -> x57, waiting for transfers between devices: none -> 134 us  [swap_over(): return lax.ppermute(values, axes, pairs)]
    dot_general x84 -> x0, matrix products: 99.7 us -> none  [the longest x25 43.3 us: dot_rows(): lax.dot_general(first_op, second_op, (((1,), (1,)), ((), ())), preferred_...]
    all_to_all x0 -> x7, blocking collectives: none -> 94.6 us  [sync(): return lax.all_to_all(copies, axes, 0, 0, tiled=True)]
    psum x2 -> x0, waiting for transfers between devices: 81.8 us -> none  [the longest x1 81.8 us: sum_gradients(): lax.psum((partial_sums[0], partial_sums[1], partial_sums[2]), 'narrow')]
    all_to_all x0 -> x7, waiting for transfers between devices: none -> 66.3 us  [sync(): return lax.all_to_all(copies, axes, 0, 0, tiled=True)]
  transfers between devices with their start and end apart: 8 -> 64, of which waited for: 4 -> 21; matrix products, arithmetic and copies ran while one was open for 13% -> 2% of each run, Pallas kernels for 0% -> 21%
where the time goes in v1:
time: 578 us; the launch traced here: 569 us
  waiting for transfers between devices  201 us (35%)
  Pallas kernels  165 us (29%)
  blocking collectives  94.6 us (16%)
  starting transfers between devices  75.8 us (13%)
  local copies, waits for them, and re-layouts  26.1 us (5%)
    pallas_call x33, Pallas kernels, call(): pl.pallas_call(kernel, out_shape=tuple(outs), in_specs=specs, out_specs=t...  165 us
    ppermute x57, waiting for transfers between devices, swap_over(): return lax.ppermute(values, axes, pairs)  134 us
    all_to_all x7, blocking collectives, sync(): return lax.all_to_all(copies, axes, 0, 0, tiled=True)  94.6 us
    all_to_all x7, waiting for transfers between devices, sync(): return lax.all_to_all(copies, axes, 0, 0, tiled=True)  66.3 us
    ppermute x57, starting transfers between devices, swap_over(): return lax.ppermute(values, axes, pairs)  51.2 us
    all_to_all x7, starting transfers between devices, sync(): return lax.all_to_all(copies, axes, 0, 0, tiled=True)  24.6 us
    unnamed x161, local copies, waits for them, and re-layouts  23.4 us
  transfers between devices with their start and end apart: 64, of which 21 were waited for; matrix products, arithmetic and copies ran while one was open for 2% of the time, Pallas kernels for 21%

profile of v1, /device:TPU:0, one launch (start us, length us, event | category | flops | bytes accessed | tf_op | source)
XLA Modules:
  0.0 568.5 jit_solution(13328563039306501535)
XLA Ops:
  1.3 5.1 shard_map.314
  6.4 7.3 %all-to-all-start = ((f32[32,16,128]{2,1,0:T(8,128)}), f32[32,16,128]{2,1,0:T(8,128)S(1)}, u32[]{:S(2)}, u32[]{:S(2)}) async-start(f32[32,16,128]{2,1,0:T(8,128)} %get-tuple-element.180), calls=%async_computation | async-start | bytes 524288 | tf_op jit(solution)/shard_map/all_to_all | solution.py:869
  15.7 8.6 %all-to-all-done.refs_0_ = f32[32,16,128]{2,1,0:T(8,128)S(1)} async-done(((f32[32,16,128]{2,1,0:T(8,128)}), f32[32,16,128]{2,1,0:T(8,128)S(1)}, u32[]{:S(2)}, u32[]{:S(2)}) %all-to-all-start) | async-done | bytes 262176 | tf_op jit(solution)/shard_map/all_to_all | solution.py:869
  25.0 9.0 %shard_map.315 = (bf16[256,512]{1,0:T(8,128)(2,1)}, bf16[256,4608]{1,0:T(8,128)(2,1)}, f32[256,4608]{1,0:T(8,128)}, f32[256,18]{1,0:T(8,128)}, f32[256,512]{1,0:...) custom-call(f32[32,16,128]{2,1,0:T(8,128)} %copy-done.9, ...), custom_call_target="tpu_custom_call" | custom-call | tf_op jit(solution)/shard_map/pallas_call | solution.py:87
  34.0 11.5 %all_to_all.70.refs_0_ = f32[32,8,128]{2,1,0:T(8,128)} all-to-all(f32[32,8,128]{2,1,0:T(8,128)} %get-tuple-element.183), channel_id=1, replica_groups=mesh['wide'=8,'narrow'=4] {'wide','narrow'}, dimensions={0} | all-to-all | bytes 262144 | tf_op jit(solution)/shard_map/all_to_all | solution.py:869
  45.5 4.2 shard_map.316
  49.7 18.9 %all_to_all.71.refs_0_ = f32[32,32,128]{2,1,0:T(8,128)} all-to-all(f32[32,32,128]{2,1,0:T(8,128)} %get-tuple-element.186), channel_id=1, replica_groups=mesh['wide'=8,'narrow'=4] {'wide','narrow'}, dimensions={0} | all-to-all | bytes 1048576 | tf_op jit(solution)/shard_map/all_to_all | solution.py:869
  68.6 6.5 %shard_map.317 = (f32[256,2048]{1,0:T(8,128)}, bf16[256,2048]{1,0:T(8,128)(2,1)}, f32[256,1024]{1,0:T(8,128)}, f32[256,512]{1,0:T(8,128)}, f32[32,8,128]{2,1,0:T(8,128)}, /*index=5*/f32[2,2048]{1,0:T(2,128)}) custom-call(f32[32,32,128]{2,1,0:T(8,128)} %all_to_all.71.refs_0_, f32[256,2048]{1,0:T(8,128)} %get-tuple-element.187.refs_1_.refs_6_.refs_2_, ...), custom_call_target="tpu_custom_call" | custom-call | tf_op jit(solution)/shard_map/pallas_call | solution.py:87
  75.1 11.5 %all_to_all.72.refs_0_ = f32[32,8,128]{2,1,0:T(8,128)} all-to-all(f32[32,8,128]{2,1,0:T(8,128)} %get-tuple-element.188), channel_id=1, replica_groups=mesh['wide'=8,'narrow'=4] {'wide','narrow'}, dimensions={0} | all-to-all | bytes 262144 | tf_op jit(solution)/shard_map/all_to_all | solution.py:869
  86.6 5.4 shard_map.318
  92.0 11.5 %all_to_all.73.refs_0_ = f32[32,8,128]{2,1,0:T(8,128)} all-to-all(f32[32,8,128]{2,1,0:T(8,128)} %get-tuple-element.190), channel_id=1, replica_groups=mesh['wide'=8,'narrow'=4] {'wide','narrow'}, dimensions={0} | all-to-all | bytes 262144 | tf_op jit(solution)/shard_map/all_to_all | solution.py:869
  103.6 4.2 shard_map.319
  107.8 2.6 all-to-all-start.5
  110.6 15.4 %all-to-all-done.5.refs_0_ = f32[32,32,128]{2,1,0:T(8,128)S(1)} async-done(((f32[32,32,128]{2,1,0:T(8,128)}), f32[32,32,128]{2,1,0:T(8,128)S(1)}, u32[]{:S(2)}, u32[]{:S(2)}) %all-to-all-start.5) | async-done | bytes 524320 | tf_op jit(solution)/shard_map/all_to_all | solution.py:869
  126.8 7.4 %shard_map.320 = (bf16[256,2048]{1,0:T(8,128)(2,1)}, f32[256,2048]{1,0:T(8,128)}, f32[32,32,128]{2,1,0:T(8,128)}, f32[2,2048]{1,0:T(2,128)}) custom-call(f32[32,32,128]{2,1,0:T(8,128)} %copy-done.1, f32[256,2048]{1,0:T(8,128)} %get-tuple-element.193.refs_1_.refs_2_, f32[256,2048]{1,0:T(8,128)} %get-tuple-element.194.refs_2_.refs_5_, ...), custom_call_target="tpu_custom_call" | custom-call | tf_op jit(solution)/shard_map/pallas_call | solution.py:87
  134.2 18.9 %all_to_all.74.refs_0_ = f32[32,32,128]{2,1,0:T(8,128)} all-to-all(f32[32,32,128]{2,1,0:T(8,128)} %get-tuple-element.196), channel_id=1, replica_groups=mesh['wide'=8,'narrow'=4] {'wide','narrow'}, dimensions={0} | all-to-all | bytes 1048576 | tf_op jit(solution)/shard_map/all_to_all | solution.py:869
  153.1 6.9 %shard_map.321 = (bf16[256,2048]{1,0:T(8,128)(2,1)}, f32[256,1024]{1,0:T(8,128)}, f32[256,512]{1,0:T(8,128)}, f32[32,8,128]{2,1,0:T(8,128)}, f32[2,2048]{1,0:T(2,128)}) custom-call(f32[32,32,128]{2,1,0:T(8,128)} %all_to_all.74.refs_0_, f32[256,2048]{1,0:T(8,128)} %get-tuple-element.197.refs_1_.refs_4_, f32[256,2048]{1,0:T(8,128)} %get-tuple-element.193.refs_1_.refs_2_, ...), custom_call_target="tpu_custom_call" | custom-call | tf_op jit(solution)/shard_map/pallas_call | solution.py:87
  160.6 11.7 %all_to_all.75.refs_0_ = f32[32,8,128]{2,1,0:T(8,128)} all-to-all(f32[32,8,128]{2,1,0:T(8,128)} %get-tuple-element.200), channel_id=1, replica_groups=mesh['wide'=8,'narrow'=4] {'wide','narrow'}, dimensions={0} | all-to-all | bytes 262144 | tf_op jit(solution)/shard_map/all_to_all | solution.py:869
  172.3 6.9 %shard_map.322 = (bf16[256,512]{1,0:T(8,128)(2,1)}, f32[256,256]{1,0:T(8,128)}, f32[256,512]{1,0:T(8,128)}, f32[32,8,128]{2,1,0:T(8,128)}, f32[2,512]{1,0:T(2,128)}) custom-call(f32[32,8,128]{2,1,0:T(8,128)} %all_to_all.75.refs_0_, f32[256,512]{1,0:T(8,128)} %get-tuple-element.201.refs_1_, f32[256,512]{1,0:T(8,128)} %get-tuple-element.191.refs_1_.refs_4_.refs_2_, ...), custom_call_target="tpu_custom_call" | custom-call | tf_op jit(solution)/shard_map/pallas_call | solution.py:87
  182.0 7.7 %shard_map.323 = (f32[8,5,32,256]{3,2,1,0:T(8,128)}, f32[8,5,32,256]{3,2,1,0:T(8,128)}, f32[8,4,32,256]{3,2,1,0:T(8,128)}, f32[8,4,32,256]{3,2,1,0:T(8,128)}, f3...) custom-call(s32[1,5]{1,0:T(1,128)} %bitcast.77, ...), custom_call_target="tpu_custom_call" | custom-call | tf_op jit(solution)/shard_map/pallas_call | solution.py:87
  191.2 3.1 all-to-all-start.8
  196.2 27.3 %all-to-all-done.8.refs_0_ = f32[32,8,128]{2,1,0:T(8,128)S(1)} async-done(((f32[32,8,128]{2,1,0:T(8,128)}), f32[32,8,128]{2,1,0:T(8,128)S(1)}, u32[]{:S(2)}, u32[]{:S(2)}) %all-to-all-start.8) | async-done | bytes 131104 | tf_op jit(solution)/shard_map/all_to_all | solution.py:869
  224.2 8.8 %shard_map.324 = (bf16[256,512]{1,0:T(8,128)(2,1)}, f32[256,512]{1,0:T(8,128)}, f32[256,2048]{1,0:T(8,128)}, f32[32,32,128]{2,1,0:T(8,128)}, f32[2,512]{1,0:T(2,128)}) custom-call(f32[32,8,128]{2,1,0:T(8,128)} %copy-done.17, f32[256,512]{1,0:T(8,128)} %get-tuple-element.204.refs_1_, f32[256,512]{1,0:T(8,128)} %get-tuple-element.189.refs_1_.refs_4_.refs_2_, ...), custom_call_target="tpu_custom_call" | custom-call | tf_op jit(solution)/shard_map/pallas_call | solution.py:87
  232.9 2.6 all-to-all-start.9
  236.1 15.0 %all-to-all-done.9.refs_0_ = f32[32,32,128]{2,1,0:T(8,128)S(1)} async-done(((f32[32,32,128]{2,1,0:T(8,128)}), f32[32,32,128]{2,1,0:T(8,128)S(1)}, u32[]{:S(2)}, u32[]{:S(2)}) %all-to-all-start.9) | async-done | bytes 524320 | tf_op jit(solution)/shard_map/all_to_all | solution.py:869
  251.9 6.7 %shard_map.325 = (bf16[256,2048]{1,0:T(8,128)(2,1)}, f32[256,1024]{1,0:T(8,128)}, f32[256,512]{1,0:T(8,128)}, f32[32,8,128]{2,1,0:T(8,128)}, f32[2,2048]{1,0:T(2,128)}) custom-call(f32[32,32,128]{2,1,0:T(8,128)} %copy-done, f32[256,2048]{1,0:T(8,128)} %get-tuple-element.215.refs_1_, f32[256,2048]{1,0:T(8,128)} %get-tuple-element.187.refs_1_.refs_6_.refs_2_, ...), custom_call_target="tpu_custom_call" | custom-call | tf_op jit(solution)/shard_map/pallas_call | solution.py:87
  259.7 5.1 shard_map.326
  267.5 11.4 %collective-permute-done.14.refs_5_ = f32[4,4,32,256]{3,2,1,0:T(8,128)} collective-permute-done((f32[4,4,32,256]{3,2,1,0:T(8,128)}, f32[4,4,32,256]{3,2,1,0:T(8,128)}, u32[]{:S(2)}, u32[]{:S(2)}) %collective-permute-start.14) | collective-permute-done | bytes 524320 | tf_op jit(solution)/shard_map/ppermute | solution.py:863
  280.7 10.7 %all_to_all.76.refs_0_ = f32[32,8,128]{2,1,0:T(8,128)} all-to-all(f32[32,8,128]{2,1,0:T(8,128)S(1)} %copy-done.45), channel_id=1, replica_groups=mesh['wide'=8,'narrow'=4] {'wide','narrow'}, dimensions={0} | all-to-all | bytes 262144 | tf_op jit(solution)/shard_map/all_to_all | solution.py:869
  291.4 11.7 %shard_map.327 = (bf16[256,512]{1,0:T(8,128)(2,1)}, f32[256,256]{1,0:T(8,128)}, f32[256,512]{1,0:T(8,128)}, f32[32,8,128]{2,1,0:T(8,128)}, f32[2,512]{1,0:T(2,128)}, /*index=5*/f32[256,512]{1,0:T(8,128)}) custom-call(f32[32,8,128]{2,1,0:T(8,128)} %all_to_all.76.refs_0_, f32[256,512]{1,0:T(8,128)} %get-tuple-element.218.refs_1_, ...), custom_call_target="tpu_custom_call" | custom-call | tf_op jit(solution)/shard_map/pallas_call | solution.py:87
  303.4 2.8 all-to-all-start.11
  306.2 3.6 shard_map.328
  310.9 11.7 %shard_map.329 = (f32[8,6,32,256]{3,2,1,0:T(8,128)}, f32[8,6,32,256]{3,2,1,0:T(8,128)}, f32[8,6,32,256]{3,2,1,0:T(8,128)}, f32[8,6,32,256]{3,2,1,0:T(8,128)}, f3...) custom-call(s32[1,5]{1,0:T(1,128)} %bitcast.82, ...), custom_call_target="tpu_custom_call" | custom-call | tf_op jit(solution)/shard_map/pallas_call | solution.py:87
  323.2 2.6 shard_map.330
  335.2 4.1 shard_map.331
  339.3 4.4 shard_map.332
  344.9 2.9 shard_map.333
  347.8 2.8 collective-permute-start.25
  350.9 25.6 %collective-permute-done.25.refs_4_ = f32[1,4,32,256]{3,2,1,0:T(8,128)S(1)} collective-permute-done((f32[1,4,32,256]{3,2,1,0:T(8,128)}, f32[1,4,32,256]{3,2,1,0:T(8,128)S(1)}, u32[]{:S(2)}, u32[]{:S(2)}) %collective-permute-start.25) | collective-permute-done | bytes 131104 | tf_op jit(solution)/shard_map/ppermute | solution.py:863
  376.5 3.3 collective-permute-start.26
  379.8 7.2 %collective-permute-done.26.refs_5_ = f32[1,4,32,256]{3,2,1,0:T(8,128)S(1)} collective-permute-done((f32[1,4,32,256]{3,2,1,0:T(8,128)}, f32[1,4,32,256]{3,2,1,0:T(8,128)S(1)}, u32[]{:S(2)}, u32[]{:S(2)}) %collective-permute-start.26) | collective-permute-done | bytes 131104 | tf_op jit(solution)/shard_map/ppermute | solution.py:863
  390.1 5.1 collective-permute-done.19.refs_5_
  398.3 3.6 collective-permute-done.20.refs_6_
  402.7 3.1 shard_map.335
  407.5 5.9 %shard_map.336 = (f32[4,6,32,256]{3,2,1,0:T(8,128)}, f32[4,6,32,256]{3,2,1,0:T(8,128)}, f32[4,6,32,256]{3,2,1,0:T(8,128)}, f32[4,6,32,256]{3,2,1,0:T(8,128)}, f3...) custom-call(s32[1,5]{1,0:T(1,128)} %bitcast.86, ...), custom_call_target="tpu_custom_call" | custom-call | tf_op jit(solution)/shard_map/pallas_call | solution.py:87
  418.2 3.3 all-to-all-start.12
  421.4 18.3 %collective-permute-done.28.refs_5_ = f32[4,1,32,256]{3,2,1,0:T(8,128)S(1)} collective-permute-done((f32[4,1,32,256]{3,2,1,0:T(8,128)}, f32[4,1,32,256]{3,2,1,0:T(8,128)S(1)}, u32[]{:S(2)}, u32[]{:S(2)}) %collective-permute-start.28) | collective-permute-done | bytes 131104 | tf_op jit(solution)/shard_map/ppermute | solution.py:863
  441.4 3.5 collective-permute-done.29.refs_6_
  445.6 2.8 shard_map.337
  450.9 4.1 shard_map.338
  460.2 3.8 collective-permute-done.35.refs_6_
  468.9 3.1 shard_map.340
  472.2 2.9 collective-permute-start.50
  478.0 2.9 all-to-all-start.13
  480.9 2.8 collective-permute-start.39
  483.9 2.8 collective-permute-start.41
  487.2 13.8 %collective-permute-done.40.refs_4_ = f32[1,1,32,256]{3,2,1,0:T(8,128)S(1)} collective-permute-done((f32[1,1,32,256]{3,2,1,0:T(8,128)S(1)}, f32[1,1,32,256]{3,2,1,0:T(8,128)S(1)}, u32[]{:S(2)}, u32[]{:S(2)}) %collective-permute-start.40) | collective-permute-done | bytes 32800 | tf_op jit(solution)/shard_map/ppermute | solution.py:863
  505.8 10.8 %collective-permute-done.49.refs_4_ = f32[1,6,32,256]{3,2,1,0:T(8,128)S(1)} collective-permute-done((f32[1,6,32,256]{3,2,1,0:T(8,128)S(1)}, f32[1,6,32,256]{3,2,1,0:T(8,128)S(1)}, u32[]{:S(2)}, u32[]{:S(2)}) %collective-permute-start.49) | collective-permute-done | bytes 196640 | tf_op jit(solution)/shard_map/ppermute | solution.py:863
  524.9 3.1 shard_map.343
  530.4 7.2 %collective-permute-done.56.refs_4_ = f32[13,32,256]{2,1,0:T(8,128)} collective-permute-done((f32[13,32,256]{2,1,0:T(8,128)S(1)}, f32[13,32,256]{2,1,0:T(8,128)}, u32[]{:S(2)}, u32[]{:S(2)}) %collective-permute-start.56) | collective-permute-done | bytes 426016 | tf_op jit(solution)/shard_map/ppermute | solution.py:863
  537.6 3.4 shard_map.346
  541.0 9.3 %collective-permute-done.52.refs_3_ = f32[17,32,256]{2,1,0:T(8,128)S(1)} collective-permute-done((f32[17,32,256]{2,1,0:T(8,128)}, f32[17,32,256]{2,1,0:T(8,128)S(1)}, u32[]{:S(2)}, u32[]{:S(2)}) %collective-permute-start.52) | collective-permute-done | bytes 557088 | tf_op jit(solution)/shard_map/ppermute | solution.py:863
  550.3 10.4 %collective-permute-done.53.refs_4_ = f32[17,32,256]{2,1,0:T(8,128)S(1)} collective-permute-done((f32[17,32,256]{2,1,0:T(8,128)}, f32[17,32,256]{2,1,0:T(8,128)S(1)}, u32[]{:S(2)}, u32[]{:S(2)}) %collective-permute-start.53) | collective-permute-done | bytes 557088 | tf_op jit(solution)/shard_map/ppermute | solution.py:863
  561.5 4.2 shard_map.345
  (286 shorter events, 80.8 us)
Async XLA Ops:
  6.4 17.9 %all-to-all-start = ((f32[32,16,128]{2,1,0:T(8,128)}), f32[32,16,128]{2,1,0:T(8,128)S(1)}, u32[]{:S(2)}, u32[]{:S(2)}) async-start(f32[32,16,128]{2,1,0:T(8,128)} %get-tuple-element.180), calls=%async_computation | async-start | bytes 524288 | tf_op jit(solution)/shard_map/all_to_all | solution.py:869
  107.8 18.2 %all-to-all-start.5 = ((f32[32,32,128]{2,1,0:T(8,128)}), f32[32,32,128]{2,1,0:T(8,128)S(1)}, u32[]{:S(2)}, u32[]{:S(2)}) async-start(f32[32,32,128]{2,1,0:T(8,128)} %get-tuple-element.192), calls=%async_computation.5 | async-start | bytes 1048576 | tf_op jit(solution)/shard_map/all_to_all | solution.py:869
  110.4 199.4 %collective-permute-start.11 = (f32[256,4608]{1,0:T(8,128)}, f32[256,4608]{1,0:T(8,128)}, u32[]{:S(2)}, u32[]{:S(2)}) collective-permute-start(f32[256,4608]{1,0:T(8,128)} %get-tuple-element.241), channel_id=1, source_target_pairs={{0,1},{1,0},{2,3},{3,2},{4,5},{5,4},{6,7},{7,6},{8,9},{9,8},{10,11... | collective-permute-start | bytes 14155784 | tf_op jit(solution)/shard_map/ppermute | solution.py:863
  159.9 21.0 %collective-permute-start.1 = (f32[256,1024]{1,0:T(8,128)}, f32[256,1024]{1,0:T(8,128)S(1)}, u32[]{:S(2)}, u32[]{:S(2)}) collective-permute-start(f32[256,1024]{1,0:T(8,128)} %get-tuple-element.209), channel_id=1, source_target_pairs={{0,1},{1,0},{2,3},{3,2},{4,5},{5,4},{6,7},{7,6},{8,9},{9,8},{10,11... | collective-permute-start | bytes 3145736 | tf_op jit(solution)/shard_map/ppermute | solution.py:863
  160.0 19.4 %collective-permute-start.2 = (f32[256,512]{1,0:T(8,128)S(1)}, f32[256,512]{1,0:T(8,128)S(1)}, u32[]{:S(2)}, u32[]{:S(2)}) collective-permute-start(f32[256,512]{1,0:T(8,128)S(1)} %copy-done.19), channel_id=1, source_target_pairs={{0,1},{1,0},{2,3},{3,2},{4,5},{5,4},{6,7},{7,6},{8,9},{9,8},{10,11... | collective-permute-start | bytes 1572872 | tf_op jit(solution)/shard_map/ppermute | solution.py:863
  160.5 18.9 %collective-permute-start = (f32[256,512]{1,0:T(8,128)S(1)}, f32[256,512]{1,0:T(8,128)S(1)}, u32[]{:S(2)}, u32[]{:S(2)}) collective-permute-start(f32[256,512]{1,0:T(8,128)S(1)} %copy-done.70), channel_id=1, source_target_pairs={{0,1},{1,0},{2,3},{3,2},{4,5},{5,4},{6,7},{7,6},{8,9},{9,8},{10,11... | collective-permute-start | bytes 1572872 | tf_op jit(solution)/shard_map/ppermute | solution.py:863
  179.2 1.8 collective-permute-start.3
  189.7 46.0 %collective-permute-start.5 = (f32[8,4,32,256]{3,2,1,0:T(8,128)}, f32[8,4,32,256]{3,2,1,0:T(8,128)}, u32[]{:S(2)}, u32[]{:S(2)}) collective-permute-start(f32[8,4,32,256]{3,2,1,0:T(8,128)} %get-tuple-element.226), channel_id=1, source_target_pairs={{0,2},{1,3},{2,0},{3,1},{4,6},{5,7},{6,4},{7,5},{8,10},{9,11},{10,... | collective-permute-start | bytes 3145736 | tf_op jit(solution)/shard_map/ppermute | solution.py:863
  190.2 68.3 %collective-permute-start.4 = (f32[8,5,32,256]{3,2,1,0:T(8,128)}, f32[8,5,32,256]{3,2,1,0:T(8,128)S(1)}, u32[]{:S(2)}, u32[]{:S(2)}) collective-permute-start(f32[8,5,32,256]{3,2,1,0:T(8,128)} %get-tuple-element.225), channel_id=1, source_target_pairs={{0,4},{1,5},{2,6},{3,7},{4,0},{5,1},{6,2},{7,3},{8,12},{9,13},{10,... | collective-permute-start | bytes 3932168 | tf_op jit(solution)/shard_map/ppermute | solution.py:863
  191.2 32.3 %all-to-all-start.8 = ((f32[32,8,128]{2,1,0:T(8,128)}), f32[32,8,128]{2,1,0:T(8,128)S(1)}, u32[]{:S(2)}, u32[]{:S(2)}) async-start(f32[32,8,128]{2,1,0:T(8,128)} %get-tuple-element.203), calls=%async_computation.8 | async-start | bytes 262144 | tf_op jit(solution)/shard_map/all_to_all | solution.py:869
  194.3 64.2 %collective-permute-start.6 = (f32[8,4,32,256]{3,2,1,0:T(8,128)}, f32[8,4,32,256]{3,2,1,0:T(8,128)}, u32[]{:S(2)}, u32[]{:S(2)}) collective-permute-start(f32[8,4,32,256]{3,2,1,0:T(8,128)} %get-tuple-element.227), channel_id=1, source_target_pairs={{0,8},{1,9},{2,10},{3,11},{4,12},{5,13},{6,14},{7,15},{8,0},{9,1},... | collective-permute-start | bytes 3145736 | tf_op jit(solution)/shard_map/ppermute | solution.py:863
  232.9 18.2 %all-to-all-start.9 = ((f32[32,32,128]{2,1,0:T(8,128)}), f32[32,32,128]{2,1,0:T(8,128)S(1)}, u32[]{:S(2)}, u32[]{:S(2)}) async-start(f32[32,32,128]{2,1,0:T(8,128)} %get-tuple-element.214), calls=%async_computation.9 | async-start | bytes 1048576 | tf_op jit(solution)/shard_map/all_to_all | solution.py:869
  235.6 31.4 %collective-permute-start.8 = (f32[256,1024]{1,0:T(8,128)}, f32[256,1024]{1,0:T(8,128)S(1)}, u32[]{:S(2)}, u32[]{:S(2)}) collective-permute-start(f32[256,1024]{1,0:T(8,128)} %get-tuple-element.235), channel_id=1, source_target_pairs={{0,1},{1,0},{2,3},{3,2},{4,5},{5,4},{6,7},{7,6},{8,9},{9,8},{10,11... | collective-permute-start | bytes 3145736 | tf_op jit(solution)/shard_map/ppermute | solution.py:863
  235.7 30.3 %collective-permute-start.9 = (f32[256,512]{1,0:T(8,128)}, f32[256,512]{1,0:T(8,128)S(1)}, u32[]{:S(2)}, u32[]{:S(2)}) collective-permute-start(f32[256,512]{1,0:T(8,128)} %get-tuple-element.237), channel_id=1, source_target_pairs={{0,1},{1,0},{2,3},{3,2},{4,5},{5,4},{6,7},{7,6},{8,9},{9,8},{10,11... | collective-permute-start | bytes 1572872 | tf_op jit(solution)/shard_map/ppermute | solution.py:863
  264.7 14.1 %collective-permute-start.14 = (f32[4,4,32,256]{3,2,1,0:T(8,128)}, f32[4,4,32,256]{3,2,1,0:T(8,128)}, u32[]{:S(2)}, u32[]{:S(2)}) collective-permute-start(f32[4,4,32,256]{3,2,1,0:T(8,128)} %get-tuple-element.248), channel_id=1, source_target_pairs={{0,8},{1,9},{2,10},{3,11},{4,12},{5,13},{6,14},{7,15},{8,0},{9,1},... | collective-permute-start | bytes 1572872 | tf_op jit(solution)/shard_map/ppermute | solution.py:863
  266.1 43.8 %collective-permute-start.10 = (f32[256,1024]{1,0:T(8,128)}, f32[256,1024]{1,0:T(8,128)S(1)}, u32[]{:S(2)}, u32[]{:S(2)}) collective-permute-start(f32[256,1024]{1,0:T(8,128)} %get-tuple-element.239), channel_id=1, source_target_pairs={{0,1},{1,0},{2,3},{3,2},{4,5},{5,4},{6,7},{7,6},{8,9},{9,8},{10,11... | collective-permute-start | bytes 3145736 | tf_op jit(solution)/shard_map/ppermute | solution.py:863
  266.1 14.7 %collective-permute-start.15 = (f32[4,4,32,256]{3,2,1,0:T(8,128)}, f32[4,4,32,256]{3,2,1,0:T(8,128)}, u32[]{:S(2)}, u32[]{:S(2)}) collective-permute-start(f32[4,4,32,256]{3,2,1,0:T(8,128)} %get-tuple-element.249), channel_id=1, source_target_pairs={{0,4},{1,5},{2,6},{3,7},{4,0},{5,1},{6,2},{7,3},{8,12},{9,13},{10,... | collective-permute-start | bytes 1572872 | tf_op jit(solution)/shard_map/ppermute | solution.py:863
  266.9 36.1 %collective-permute-start.13 = (f32[4,5,32,256]{3,2,1,0:T(8,128)}, f32[4,5,32,256]{3,2,1,0:T(8,128)S(1)}, u32[]{:S(2)}, u32[]{:S(2)}) collective-permute-start(f32[4,5,32,256]{3,2,1,0:T(8,128)} %get-tuple-element.247), channel_id=1, source_target_pairs={{0,2},{1,3},{2,0},{3,1},{4,6},{5,7},{6,4},{7,5},{8,10},{9,11},{10,... | collective-permute-start | bytes 1966088 | tf_op jit(solution)/shard_map/ppermute | solution.py:863
  278.8 31.0 %collective-permute-start.7 = (f32[256,512]{1,0:T(8,128)}, f32[256,512]{1,0:T(8,128)}, u32[]{:S(2)}, u32[]{:S(2)}) collective-permute-start(f32[256,512]{1,0:T(8,128)} %get-tuple-element.233), channel_id=1, source_target_pairs={{0,1},{1,0},{2,3},{3,2},{4,5},{5,4},{6,7},{7,6},{8,9},{9,8},{10,11... | collective-permute-start | bytes 1572872 | tf_op jit(solution)/shard_map/ppermute | solution.py:863
  280.7 50.1 %collective-permute-start.17 = (f32[256,1024]{1,0:T(8,128)}, f32[256,1024]{1,0:T(8,128)}, u32[]{:S(2)}, u32[]{:S(2)}) collective-permute-start(f32[256,1024]{1,0:T(8,128)} %get-tuple-element.256), channel_id=1, source_target_pairs={{0,1},{1,0},{2,3},{3,2},{4,5},{5,4},{6,7},{7,6},{8,9},{9,8},{10,11... | collective-permute-start | bytes 3145736 | tf_op jit(solution)/shard_map/ppermute | solution.py:863
  303.1 6.7 %collective-permute-start.12 = (f32[256,256]{1,0:T(8,128)}, f32[256,256]{1,0:T(8,128)S(1)}, u32[]{:S(2)}, u32[]{:S(2)}) collective-permute-start(f32[256,256]{1,0:T(8,128)} %get-tuple-element.243), channel_id=1, source_target_pairs={{0,1},{1,0},{2,3},{3,2},{4,5},{5,4},{6,7},{7,6},{8,9},{9,8},{10,11... | collective-permute-start | bytes 786440 | tf_op jit(solution)/shard_map/ppermute | solution.py:863
  303.4 19.2 %all-to-all-start.11 = ((f32[32,8,128]{2,1,0:T(8,128)}), f32[32,8,128]{2,1,0:T(8,128)S(1)}, u32[]{:S(2)}, u32[]{:S(2)}) async-start(f32[32,8,128]{2,1,0:T(8,128)} %get-tuple-element.230), calls=%async_computation.11 | async-start | bytes 262144 | tf_op jit(solution)/shard_map/all_to_all | solution.py:869
  325.8 5.6 collective-permute-start.16
  326.1 18.1 %collective-permute-start.21 = (f32[2,5,32,256]{3,2,1,0:T(8,128)}, f32[2,5,32,256]{3,2,1,0:T(8,128)S(1)}, u32[]{:S(2)}, u32[]{:S(2)}) collective-permute-start(f32[2,5,32,256]{3,2,1,0:T(8,128)} %get-tuple-element.267), channel_id=1, source_target_pairs={{0,8},{1,9},{2,10},{3,11},{4,12},{5,13},{6,14},{7,15},{8,0},{9,1},... | collective-permute-start | bytes 983048 | tf_op jit(solution)/shard_map/ppermute | solution.py:863
  327.8 16.0 %collective-permute-start.22 = (f32[2,4,32,256]{3,2,1,0:T(8,128)}, f32[2,4,32,256]{3,2,1,0:T(8,128)}, u32[]{:S(2)}, u32[]{:S(2)}) collective-permute-start(f32[2,4,32,256]{3,2,1,0:T(8,128)} %get-tuple-element.268), channel_id=1, source_target_pairs={{0,4},{1,5},{2,6},{3,7},{4,0},{5,1},{6,2},{7,3},{8,12},{9,13},{10,... | collective-permute-start | bytes 786440 | tf_op jit(solution)/shard_map/ppermute | solution.py:863
  329.3 14.9 %collective-permute-start.23 = (f32[2,4,32,256]{3,2,1,0:T(8,128)}, f32[2,4,32,256]{3,2,1,0:T(8,128)}, u32[]{:S(2)}, u32[]{:S(2)}) collective-permute-start(f32[2,4,32,256]{3,2,1,0:T(8,128)} %get-tuple-element.269), channel_id=1, source_target_pairs={{0,2},{1,3},{2,0},{3,1},{4,6},{5,7},{6,4},{7,5},{8,10},{9,11},{10,... | collective-permute-start | bytes 786440 | tf_op jit(solution)/shard_map/ppermute | solution.py:863
  330.8 75.0 %collective-permute-start.30 = (f32[8,6,32,256]{3,2,1,0:T(8,128)}, f32[8,6,32,256]{3,2,1,0:T(8,128)S(1)}, u32[]{:S(2)}, u32[]{:S(2)}) collective-permute-start(f32[8,6,32,256]{3,2,1,0:T(8,128)} %get-tuple-element.288), channel_id=1, source_target_pairs={{0,4},{1,5},{2,6},{3,7},{4,0},{5,1},{6,2},{7,3},{8,12},{9,13},{10,... | collective-permute-start | bytes 4718600 | tf_op jit(solution)/shard_map/ppermute | solution.py:863
  332.2 73.6 %collective-permute-start.31 = (f32[8,6,32,256]{3,2,1,0:T(8,128)}, f32[8,6,32,256]{3,2,1,0:T(8,128)S(1)}, u32[]{:S(2)}, u32[]{:S(2)}) collective-permute-start(f32[8,6,32,256]{3,2,1,0:T(8,128)} %get-tuple-element.289), channel_id=1, source_target_pairs={{0,2},{1,3},{2,0},{3,1},{4,6},{5,7},{6,4},{7,5},{8,10},{9,11},{10,... | collective-permute-start | bytes 4718600 | tf_op jit(solution)/shard_map/ppermute | solution.py:863
  343.8 62.0 %collective-permute-start.32 = (f32[8,5,32,256]{3,2,1,0:T(8,128)}, f32[8,5,32,256]{3,2,1,0:T(8,128)}, u32[]{:S(2)}, u32[]{:S(2)}) collective-permute-start(f32[8,5,32,256]{3,2,1,0:T(8,128)} %get-tuple-element.290), channel_id=1, source_target_pairs={{0,8},{1,9},{2,10},{3,11},{4,12},{5,13},{6,14},{7,15},{8,0},{9,1},... | collective-permute-start | bytes 3932168 | tf_op jit(solution)/shard_map/ppermute | solution.py:863
  347.8 28.6 %collective-permute-start.25 = (f32[1,4,32,256]{3,2,1,0:T(8,128)}, f32[1,4,32,256]{3,2,1,0:T(8,128)S(1)}, u32[]{:S(2)}, u32[]{:S(2)}) collective-permute-start(f32[1,4,32,256]{3,2,1,0:T(8,128)} %get-tuple-element.275), channel_id=1, source_target_pairs={{0,16},{1,17},{2,18},{3,19},{4,20},{5,21},{6,22},{7,23},{8,24},{9,... | collective-permute-start | bytes 393224 | tf_op jit(solution)/shard_map/ppermute | solution.py:863
  350.6 37.9 %collective-permute-start.24 = (f32[1,5,32,256]{3,2,1,0:T(8,128)}, f32[1,5,32,256]{3,2,1,0:T(8,128)S(1)}, u32[]{:S(2)}, u32[]{:S(2)}) collective-permute-start(f32[1,5,32,256]{3,2,1,0:T(8,128)} %get-tuple-element.274), channel_id=1, source_target_pairs={{0,16},{1,17},{2,18},{3,19},{4,20},{5,21},{6,22},{7,23},{8,24},{9,... | collective-permute-start | bytes 491528 | tf_op jit(solution)/shard_map/ppermute | solution.py:863
  376.5 10.5 %collective-permute-start.26 = (f32[1,4,32,256]{3,2,1,0:T(8,128)}, f32[1,4,32,256]{3,2,1,0:T(8,128)S(1)}, u32[]{:S(2)}, u32[]{:S(2)}) collective-permute-start(f32[1,4,32,256]{3,2,1,0:T(8,128)} %get-tuple-element.276), channel_id=1, source_target_pairs={{0,16},{1,17},{2,18},{3,19},{4,20},{5,21},{6,22},{7,23},{8,24},{9,... | collective-permute-start | bytes 393224 | tf_op jit(solution)/shard_map/ppermute | solution.py:863
  387.0 14.9 %collective-permute-start.18 = (f32[8,2,32,256]{3,2,1,0:T(8,128)}, f32[8,2,32,256]{3,2,1,0:T(8,128)S(1)}, u32[]{:S(2)}, u32[]{:S(2)}) collective-permute-start(f32[8,2,32,256]{3,2,1,0:T(8,128)} %get-tuple-element.261), channel_id=1, source_target_pairs={{0,4},{1,5},{2,6},{3,7},{4,0},{5,1},{6,2},{7,3},{8,12},{9,13},{10,... | collective-permute-start | bytes 1572872 | tf_op jit(solution)/shard_map/ppermute | solution.py:863
  388.5 6.6 %collective-permute-start.19 = (f32[8,1,32,256]{3,2,1,0:T(8,128)}, f32[8,1,32,256]{3,2,1,0:T(8,128)S(1)}, u32[]{:S(2)}, u32[]{:S(2)}) collective-permute-start(f32[8,1,32,256]{3,2,1,0:T(8,128)} %get-tuple-element.262), channel_id=1, source_target_pairs={{0,2},{1,3},{2,0},{3,1},{4,6},{5,7},{6,4},{7,5},{8,10},{9,11},{10,... | collective-permute-start | bytes 786440 | tf_op jit(solution)/shard_map/ppermute | solution.py:863
  395.2 6.7 %collective-permute-start.20 = (f32[8,1,32,256]{3,2,1,0:T(8,128)}, f32[8,1,32,256]{3,2,1,0:T(8,128)}, u32[]{:S(2)}, u32[]{:S(2)}) collective-permute-start(f32[8,1,32,256]{3,2,1,0:T(8,128)} %get-tuple-element.263), channel_id=1, source_target_pairs={{0,8},{1,9},{2,10},{3,11},{4,12},{5,13},{6,14},{7,15},{8,0},{9,1},... | collective-permute-start | bytes 786440 | tf_op jit(solution)/shard_map/ppermute | solution.py:863
  413.3 36.2 %collective-permute-start.36 = (f32[4,6,32,256]{3,2,1,0:T(8,128)}, f32[4,6,32,256]{3,2,1,0:T(8,128)S(1)}, u32[]{:S(2)}, u32[]{:S(2)}) collective-permute-start(f32[4,6,32,256]{3,2,1,0:T(8,128)} %get-tuple-element.302), channel_id=1, source_target_pairs={{0,2},{1,3},{2,0},{3,1},{4,6},{5,7},{6,4},{7,5},{8,10},{9,11},{10,... | collective-permute-start | bytes 2359304 | tf_op jit(solution)/shard_map/ppermute | solution.py:863
  414.9 34.6 %collective-permute-start.37 = (f32[4,6,32,256]{3,2,1,0:T(8,128)}, f32[4,6,32,256]{3,2,1,0:T(8,128)S(1)}, u32[]{:S(2)}, u32[]{:S(2)}) collective-permute-start(f32[4,6,32,256]{3,2,1,0:T(8,128)} %get-tuple-element.303), channel_id=1, source_target_pairs={{0,8},{1,9},{2,10},{3,11},{4,12},{5,13},{6,14},{7,15},{8,0},{9,1},... | collective-permute-start | bytes 2359304 | tf_op jit(solution)/shard_map/ppermute | solution.py:863
  415.3 29.6 %collective-permute-start.27 = (f32[4,2,32,256]{3,2,1,0:T(8,128)S(1)}, f32[4,2,32,256]{3,2,1,0:T(8,128)S(1)}, u32[]{:S(2)}, u32[]{:S(2)}) collective-permute-start(f32[4,2,32,256]{3,2,1,0:T(8,128)S(1)} %copy-done.71), channel_id=1, source_target_pairs={{0,2},{1,3},{2,0},{3,1},{4,6},{5,7},{6,4},{7,5},{8,10},{9,11},{10,... | collective-permute-start | bytes 786440 | tf_op jit(solution)/shard_map/ppermute | solution.py:863
  415.9 23.8 %collective-permute-start.28 = (f32[4,1,32,256]{3,2,1,0:T(8,128)}, f32[4,1,32,256]{3,2,1,0:T(8,128)S(1)}, u32[]{:S(2)}, u32[]{:S(2)}) collective-permute-start(f32[4,1,32,256]{3,2,1,0:T(8,128)} %get-tuple-element.283), channel_id=1, source_target_pairs={{0,8},{1,9},{2,10},{3,11},{4,12},{5,13},{6,14},{7,15},{8,0},{9,1},... | collective-permute-start | bytes 393224 | tf_op jit(solution)/shard_map/ppermute | solution.py:863
  417.5 32.0 %collective-permute-start.38 = (f32[4,5,32,256]{3,2,1,0:T(8,128)}, f32[4,5,32,256]{3,2,1,0:T(8,128)S(1)}, u32[]{:S(2)}, u32[]{:S(2)}) collective-permute-start(f32[4,5,32,256]{3,2,1,0:T(8,128)} %get-tuple-element.304), channel_id=1, source_target_pairs={{0,4},{1,5},{2,6},{3,7},{4,0},{5,1},{6,2},{7,3},{8,12},{9,13},{10,... | collective-permute-start | bytes 1966088 | tf_op jit(solution)/shard_map/ppermute | solution.py:863
  418.2 56.9 %all-to-all-start.12 = ((f32[32,8,512]{2,1,0:T(8,128)}), f32[32,8,512]{2,1,0:T(8,128)S(1)}, u32[]{:S(2)}, u32[]{:S(2)}) async-start(f32[32,8,512]{2,1,0:T(8,128)} %bitcast.49), calls=%async_computation.12 | async-start | bytes 1048576 | tf_op jit(solution)/shard_map/all_to_all | solution.py:869
  439.7 5.2 collective-permute-start.29
  448.4 10.5 %collective-permute-start.34 = (f32[2,1,32,256]{3,2,1,0:T(8,128)}, f32[2,1,32,256]{3,2,1,0:T(8,128)S(1)}, u32[]{:S(2)}, u32[]{:S(2)}) collective-permute-start(f32[2,1,32,256]{3,2,1,0:T(8,128)} %get-tuple-element.297), channel_id=1, source_target_pairs={{0,4},{1,5},{2,6},{3,7},{4,0},{5,1},{6,2},{7,3},{8,12},{9,13},{10,... | collective-permute-start | bytes 196616 | tf_op jit(solution)/shard_map/ppermute | solution.py:863
  455.0 13.0 %collective-permute-start.42 = (f32[2,6,32,256]{3,2,1,0:T(8,128)}, f32[2,6,32,256]{3,2,1,0:T(8,128)S(1)}, u32[]{:S(2)}, u32[]{:S(2)}) collective-permute-start(f32[2,6,32,256]{3,2,1,0:T(8,128)} %get-tuple-element.316), channel_id=1, source_target_pairs={{0,8},{1,9},{2,10},{3,11},{4,12},{5,13},{6,14},{7,15},{8,0},{9,1},... | collective-permute-start | bytes 1179656 | tf_op jit(solution)/shard_map/ppermute | solution.py:863
  455.1 12.9 %collective-permute-start.43 = (f32[2,6,32,256]{3,2,1,0:T(8,128)}, f32[2,6,32,256]{3,2,1,0:T(8,128)S(1)}, u32[]{:S(2)}, u32[]{:S(2)}) collective-permute-start(f32[2,6,32,256]{3,2,1,0:T(8,128)} %get-tuple-element.317), channel_id=1, source_target_pairs={{0,4},{1,5},{2,6},{3,7},{4,0},{5,1},{6,2},{7,3},{8,12},{9,13},{10,... | collective-permute-start | bytes 1179656 | tf_op jit(solution)/shard_map/ppermute | solution.py:863
  456.1 11.8 %collective-permute-start.44 = (f32[2,5,32,256]{3,2,1,0:T(8,128)}, f32[2,5,32,256]{3,2,1,0:T(8,128)S(1)}, u32[]{:S(2)}, u32[]{:S(2)}) collective-permute-start(f32[2,5,32,256]{3,2,1,0:T(8,128)} %get-tuple-element.318), channel_id=1, source_target_pairs={{0,2},{1,3},{2,0},{3,1},{4,6},{5,7},{6,4},{7,5},{8,10},{9,11},{10,... | collective-permute-start | bytes 983048 | tf_op jit(solution)/shard_map/ppermute | solution.py:863
  456.8 7.9 %collective-permute-start.33 = (f32[2,2,32,256]{3,2,1,0:T(8,128)S(1)}, f32[2,2,32,256]{3,2,1,0:T(8,128)S(1)}, u32[]{:S(2)}, u32[]{:S(2)}) collective-permute-start(f32[2,2,32,256]{3,2,1,0:T(8,128)S(1)} %copy-done.73), channel_id=1, source_target_pairs={{0,8},{1,9},{2,10},{3,11},{4,12},{5,13},{6,14},{7,15},{8,0},{9,1},... | collective-permute-start | bytes 393224 | tf_op jit(solution)/shard_map/ppermute | solution.py:863
  458.8 5.2 collective-permute-start.35
  472.1 33.6 %collective-permute-start.48 = (f32[1,6,32,256]{3,2,1,0:T(8,128)}, f32[1,6,32,256]{3,2,1,0:T(8,128)S(1)}, u32[]{:S(2)}, u32[]{:S(2)}) collective-permute-start(f32[1,6,32,256]{3,2,1,0:T(8,128)} %get-tuple-element.325), channel_id=1, source_target_pairs={{0,16},{1,17},{2,18},{3,19},{4,20},{5,21},{6,22},{7,23},{8,24},{9,... | collective-permute-start | bytes 589832 | tf_op jit(solution)/shard_map/ppermute | solution.py:863
  472.2 33.3 %collective-permute-start.50 = (f32[1,5,32,256]{3,2,1,0:T(8,128)}, f32[1,5,32,256]{3,2,1,0:T(8,128)S(1)}, u32[]{:S(2)}, u32[]{:S(2)}) collective-permute-start(f32[1,5,32,256]{3,2,1,0:T(8,128)} %get-tuple-element.327), channel_id=1, source_target_pairs={{0,16},{1,17},{2,18},{3,19},{4,20},{5,21},{6,22},{7,23},{8,24},{9,... | collective-permute-start | bytes 491528 | tf_op jit(solution)/shard_map/ppermute | solution.py:863
  478.0 46.1 %all-to-all-start.13 = ((f32[32,8,512]{2,1,0:T(8,128)}), f32[32,8,512]{2,1,0:T(8,128)S(1)}, u32[]{:S(2)}, u32[]{:S(2)}) async-start(f32[32,8,512]{2,1,0:T(8,128)} %shard_map.344), calls=%async_computation.13 | async-start | bytes 1048576 | tf_op jit(solution)/shard_map/all_to_all | solution.py:869
  480.9 20.6 %collective-permute-start.39 = (f32[1,2,32,256]{3,2,1,0:T(8,128)S(1)}, f32[1,2,32,256]{3,2,1,0:T(8,128)S(1)}, u32[]{:S(2)}, u32[]{:S(2)}) collective-permute-start(f32[1,2,32,256]{3,2,1,0:T(8,128)S(1)} %copy-done.74), channel_id=1, source_target_pairs={{0,16},{1,17},{2,18},{3,19},{4,20},{5,21},{6,22},{7,23},{8,24},{9,... | collective-permute-start | bytes 196616 | tf_op jit(solution)/shard_map/ppermute | solution.py:863
  483.7 17.4 %collective-permute-start.40 = (f32[1,1,32,256]{3,2,1,0:T(8,128)S(1)}, f32[1,1,32,256]{3,2,1,0:T(8,128)S(1)}, u32[]{:S(2)}, u32[]{:S(2)}) collective-permute-start(f32[1,1,32,256]{3,2,1,0:T(8,128)S(1)} %copy-done.77), channel_id=1, source_target_pairs={{0,16},{1,17},{2,18},{3,19},{4,20},{5,21},{6,22},{7,23},{8,24},{9,... | collective-permute-start | bytes 98312 | tf_op jit(solution)/shard_map/ppermute | solution.py:863
  483.9 17.6 %collective-permute-start.41 = (f32[1,1,32,256]{3,2,1,0:T(8,128)S(1)}, f32[1,1,32,256]{3,2,1,0:T(8,128)S(1)}, u32[]{:S(2)}, u32[]{:S(2)}) collective-permute-start(f32[1,1,32,256]{3,2,1,0:T(8,128)S(1)} %copy-done.76), channel_id=1, source_target_pairs={{0,16},{1,17},{2,18},{3,19},{4,20},{5,21},{6,22},{7,23},{8,24},{9,... | collective-permute-start | bytes 98312 | tf_op jit(solution)/shard_map/ppermute | solution.py:863
  501.1 19.5 %collective-permute-start.54 = (f32[13,32,256]{2,1,0:T(8,128)S(1)}, f32[13,32,256]{2,1,0:T(8,128)S(1)}, u32[]{:S(2)}, u32[]{:S(2)}) collective-permute-start(f32[13,32,256]{2,1,0:T(8,128)S(1)} %copy-done.25), channel_id=1, source_target_pairs={{0,1},{1,0},{2,3},{3,2},{4,5},{5,4},{6,7},{7,6},{8,9},{9,8},{10,11... | collective-permute-start | bytes 1277960 | tf_op jit(solution)/shard_map/ppermute | solution.py:863
  503.7 17.3 %collective-permute-start.45 = (f32[4,32,256]{2,1,0:T(8,128)}, f32[4,32,256]{2,1,0:T(8,128)S(1)}, u32[]{:S(2)}, u32[]{:S(2)}) collective-permute-start(f32[4,32,256]{2,1,0:T(8,128)} %get-tuple-element.321.refs_1_), channel_id=1, source_target_pairs={{0,1},{1,0},{2,3},{3,2},{4,5},{5,4},{6,7},{7,6},{8,9},{9,8},{10,11... | collective-permute-start | bytes 393224 | tf_op jit(solution)/shard_map/ppermute | solution.py:863
  504.0 17.5 %collective-permute-start.46 = (f32[4,32,256]{2,1,0:T(8,128)}, f32[4,32,256]{2,1,0:T(8,128)S(1)}, u32[]{:S(2)}, u32[]{:S(2)}) collective-permute-start(f32[4,32,256]{2,1,0:T(8,128)} %get-tuple-element.321.refs_1_), channel_id=1, source_target_pairs={{0,2},{1,3},{2,0},{3,1},{4,6},{5,7},{6,4},{7,5},{8,10},{9,11},{10,... | collective-permute-start | bytes 393224 | tf_op jit(solution)/shard_map/ppermute | solution.py:863
  505.5 17.3 %collective-permute-start.47 = (f32[4,32,256]{2,1,0:T(8,128)}, f32[4,32,256]{2,1,0:T(8,128)S(1)}, u32[]{:S(2)}, u32[]{:S(2)}) collective-permute-start(f32[4,32,256]{2,1,0:T(8,128)} %get-tuple-element.321.refs_1_), channel_id=1, source_target_pairs={{0,3},{1,2},{2,1},{3,0},{4,7},{5,6},{6,5},{7,4},{8,11},{9,10},{10,... | collective-permute-start | bytes 393224 | tf_op jit(solution)/shard_map/ppermute | solution.py:863
  505.7 10.9 %collective-permute-start.49 = (f32[1,6,32,256]{3,2,1,0:T(8,128)S(1)}, f32[1,6,32,256]{3,2,1,0:T(8,128)S(1)}, u32[]{:S(2)}, u32[]{:S(2)}) collective-permute-start(f32[1,6,32,256]{3,2,1,0:T(8,128)S(1)} %copy-done.72), channel_id=1, source_target_pairs={{0,16},{1,17},{2,18},{3,19},{4,20},{5,21},{6,22},{7,23},{8,24},{9,... | collective-permute-start | bytes 589832 | tf_op jit(solution)/shard_map/ppermute | solution.py:863
  516.6 13.8 %collective-permute-start.55 = (f32[13,32,256]{2,1,0:T(8,128)S(1)}, f32[13,32,256]{2,1,0:T(8,128)}, u32[]{:S(2)}, u32[]{:S(2)}) collective-permute-start(f32[13,32,256]{2,1,0:T(8,128)S(1)} %copy-done.25), channel_id=1, source_target_pairs={{0,2},{1,3},{2,0},{3,1},{4,6},{5,7},{6,4},{7,5},{8,10},{9,11},{10,... | collective-permute-start | bytes 1277960 | tf_op jit(solution)/shard_map/ppermute | solution.py:863
  520.6 17.0 %collective-permute-start.56 = (f32[13,32,256]{2,1,0:T(8,128)S(1)}, f32[13,32,256]{2,1,0:T(8,128)}, u32[]{:S(2)}, u32[]{:S(2)}) collective-permute-start(f32[13,32,256]{2,1,0:T(8,128)S(1)} %copy-done.25), channel_id=1, source_target_pairs={{0,3},{1,2},{2,1},{3,0},{4,7},{5,6},{6,5},{7,4},{8,11},{9,10},{10,... | collective-permute-start | bytes 1277960 | tf_op jit(solution)/shard_map/ppermute | solution.py:863
  521.0 20.0 %collective-permute-start.51 = (f32[17,32,256]{2,1,0:T(8,128)}, f32[17,32,256]{2,1,0:T(8,128)S(1)}, u32[]{:S(2)}, u32[]{:S(2)}) collective-permute-start(f32[17,32,256]{2,1,0:T(8,128)} %get-tuple-element.332.refs_1_), channel_id=1, source_target_pairs={{0,1},{1,0},{2,3},{3,2},{4,5},{5,4},{6,7},{7,6},{8,9},{9,8},{10,11... | collective-permute-start | bytes 1671176 | tf_op jit(solution)/shard_map/ppermute | solution.py:863
  521.5 28.9 %collective-permute-start.52 = (f32[17,32,256]{2,1,0:T(8,128)}, f32[17,32,256]{2,1,0:T(8,128)S(1)}, u32[]{:S(2)}, u32[]{:S(2)}) collective-permute-start(f32[17,32,256]{2,1,0:T(8,128)} %get-tuple-element.332.refs_1_), channel_id=1, source_target_pairs={{0,2},{1,3},{2,0},{3,1},{4,6},{5,7},{6,4},{7,5},{8,10},{9,11},{10,... | collective-permute-start | bytes 1671176 | tf_op jit(solution)/shard_map/ppermute | solution.py:863
  522.8 37.9 %collective-permute-start.53 = (f32[17,32,256]{2,1,0:T(8,128)}, f32[17,32,256]{2,1,0:T(8,128)S(1)}, u32[]{:S(2)}, u32[]{:S(2)}) collective-permute-start(f32[17,32,256]{2,1,0:T(8,128)} %get-tuple-element.332.refs_1_), channel_id=1, source_target_pairs={{0,3},{1,2},{2,1},{3,0},{4,7},{5,6},{6,5},{7,4},{8,11},{9,10},{10,... | collective-permute-start | bytes 1671176 | tf_op jit(solution)/shard_map/ppermute | solution.py:863
  (79 other events, 891.7 us)
